TPU v7x, 512 devices: a whole 4x8x8 slice. The times are simulated.
512 devices in a mesh: tracer: 32 (over y, z_hi, core), space: 16 (over z_lo, x).
Axes of the slice: x: 4, y: 8, z: 8 (z_hi: 2, z_lo: 4; z = z_hi * 4 + z_lo), core: 2. Of those that a mesh axis runs over, the one named last changes fastest.
Arguments:
- tracers: float32 [256, 4, 384, 256], P('tracer', None, 'space'), may hold values from -6 to 6
- thickness: float32 [4, 384, 256], P(None, 'space', 'tracer'), may hold values from 0.5 to 1.5
- wind_x: float32 [4, 384, 256], P(None, 'space', 'tracer'), may hold values from -3 to 3
- wind_y: float32 [4, 384, 256], P(None, 'space', 'tracer'), may hold values from -3 to 3
Outputs:
- tracers_out: float32 [256, 4, 384, 256], P('tracer', None, 'space')
- thickness_out: float32 [4, 384, 256], P(None, 'space', 'tracer')
All inputs are finite; a program needn't handle non-finite values.
Results may differ from a plain program's by a relative error of at most 0.0003.
Values sent between devices are 32-bit elements; how exact they have to be, the bound alone decides.
No kernel may reach another device: no remote copies, remote signals or barrier semaphores. Data moves between devices by JAX's collectives and lax.ppermute only.
A program may use at most 64 MiB of HBM per device.

v0:
```python
import jax
import jax.numpy as jnp
from jax import lax
from jax.sharding import PartitionSpec as P

SUBSTEPS = 2


courant_scale = 0.025


def extended(cells, sides, width):
    for axis, dim in sides:
        count = lax.axis_size(axis)
        ends = count - 1
        head = lax.slice_in_dim(cells, 0, width, axis=dim)
        tail = lax.slice_in_dim(cells, cells.shape[dim] - width, cells.shape[dim], axis=dim)
        cells = jnp.concatenate(
            [
                lax.ppermute(tail, axis, [(i, (i + 1) % count) for i in range(ends)]),
                cells,
                lax.ppermute(head, axis, [((i + 1) % count, i) for i in range(ends)]),
            ],
            axis=dim,
        )
    return cells


def from_behind(block, axis, distance):
    devices = range(lax.axis_size(axis))
    route = [(i - distance, i) for i in devices if i - distance in devices]
    return lax.ppermute(block, axis, route)


def slab(array, start, size, axis):
    index = [slice(None)] * array.ndim
    index[axis] = slice(start, start + size)
    return array[tuple(index)]


def face_values(padded, courant, count, axis):
    width = count + 3
    edges = 7.0 / 12.0 * (
        slab(padded, 1, width, axis) + slab(padded, 2, width, axis)
    ) - 1.0 / 12.0 * (slab(padded, 0, width, axis) + slab(padded, 3, width, axis))
    left_low = slab(edges, 0, count + 1, axis)
    left_high = slab(edges, 1, count + 1, axis)
    left_mean = slab(padded, 2, count + 1, axis)
    right_low = slab(edges, 1, count + 1, axis)
    right_high = slab(edges, 2, count + 1, axis)
    right_mean = slab(padded, 3, count + 1, axis)
    left_curve = 6.0 * left_mean - 3.0 * (left_low + left_high)
    right_curve = 6.0 * right_mean - 3.0 * (right_low + right_high)
    upwind_pos = left_high - 0.5 * courant * (
        left_high - left_low - (1.0 - courant * (2.0 / 3.0)) * left_curve
    )
    upwind_neg = right_low - 0.5 * courant * (
        right_high - right_low + (1.0 + courant * (2.0 / 3.0)) * right_curve
    )
    return jnp.where(courant > 0, upwind_pos, upwind_neg)


def thin_out(thick, mass_flux, axis):
    count = thick.shape[axis]
    return thick - (slab(mass_flux, 1, count, axis) - slab(mass_flux, 0, count, axis))


def sweep(values, thick_old, thick_new, courant, mass_flux, padded, axis):
    count = values.shape[axis]
    flux = mass_flux * face_values(padded, courant, count, axis)
    change = slab(flux, 1, count, axis) - slab(flux, 0, count, axis)
    return (values * thick_old - change) / thick_new


def face_fields(rows, below, row_start, row_total, col_start):
    thick_rows = rows[0]
    cells = rows.shape[2] - 2
    width = rows.shape[3]
    thick = thick_rows[:, 1:-1]
    row_index = lax.broadcasted_iota(jnp.int32, (cells + 1, 1), 0) + row_start
    open_rows = (row_index > 0) & (row_index < row_total)
    cx = jnp.where(open_rows, courant_scale * rows[1][:, 1:], jnp.float32(0.0))
    mfx = cx * jnp.where(cx > 0, thick_rows[:, :-1], thick_rows[:, 1:])
    col_index = lax.broadcasted_iota(jnp.int32, (1, width), 1) + col_start
    cy = jnp.where(col_index > 0, courant_scale * rows[2][:, 1:-1], jnp.float32(0.0))
    mfy = cy * jnp.where(cy > 0, below, thick)
    return (cx, mfx, cy, mfy, thick)


def close_cols(field):
    closing = jnp.zeros(field.shape[:2] + (1,), jnp.float32)
    return jnp.concatenate([field, closing], axis=2)


def per_device(tracers, thickness, wind_x, wind_y):
    cells = thickness.shape[1]
    block = thickness.shape[2]
    space_count = lax.axis_size("space")
    space_pos = lax.axis_index("space")
    tracer_pos = lax.axis_index("tracer")
    stacked = jnp.stack([thickness, wind_x, wind_y])
    padded = extended(stacked, (("space", 2),), 1)
    lower_col = from_behind(thickness[:, :, block - 1 :], "tracer", 1)
    below = jnp.concatenate([lower_col, thickness[:, :, : block - 1]], axis=2)
    cx, mfx, cy, mfy, thick = face_fields(
        padded, below, space_pos * cells, space_count * cells, tracer_pos * block
    )
    row_faces, col_faces = (
        lax.all_gather(jnp.stack([cx, mfx]), "tracer", axis=3, tiled=True),
        lax.all_gather(jnp.stack([cy, mfy, thick]), "tracer", axis=3, tiled=True),
    )
    cx, mfx = (row_faces[0], row_faces[1])
    cy, mfy, thick = (col_faces[0], col_faces[1], col_faces[2])
    values = tracers
    cy = close_cols(cy)
    mfy = close_cols(mfy)
    for step in range(SUBSTEPS):
        after_x = thin_out(thick, mfx, -2)
        padded_rows = extended(values, (("space", 2),), 3)
        values = sweep(values, thick, after_x, cx, mfx, padded_rows, -2)
        after_y = thin_out(after_x, mfy, -1)
        padded_cols = jnp.pad(values, ((0, 0), (0, 0), (0, 0), (3, 3)))
        values = sweep(values, after_x, after_y, cy, mfy, padded_cols, -1)
        thick = after_y
    thick_block = lax.dynamic_slice_in_dim(thick, tracer_pos * block, block, 2)
    return (values, thick_block)


def solution(mesh):
    in_specs = (
        P("tracer", None, "space", None),
        P(None, "space", "tracer"),
        P(None, "space", "tracer"),
        P(None, "space", "tracer"),
    )
    out_specs = (P("tracer", None, "space", None), P(None, "space", "tracer"))
    return jax.shard_map(
        per_device, mesh=mesh, in_specs=in_specs, out_specs=out_specs, check_vma=False
    )
```

profile of v0, /device:TPU:30, one launch (start us, length us, event | category | flops | bytes accessed | tf_op | source)
XLA Modules:
  0.0 192.3 jit_solution(4131122415923662219)
XLA Ops:
  1.6 4.2 %collective-permute-start = (f32[3,4,1,8]{2,3,1,0:T(8,128)S(1)}, f32[3,4,1,8]{2,3,1,0:T(8,128)S(1)}, u32[]{:S(2)}, u32[]{:S(2)}) collective-permute-start(f32[3,4,1,8]{2,3,1,0:T(8,128)S(1)} %get-tuple-element.27), channel_id=1, source_target_pairs={{0,1},{1,2},{2,3},{3,4},{4,5},{5,6},{6,7},{7,8},{8,9},{9,10},{10,1... | collective-permute-start | bytes 1160 | tf_op jit(solution)/shard_map/ppermute | solution.py:20
  5.8 1.9 collective-permute-start.1
  8.4 1.9 collective-permute-start.2
  10.3 1.8 fusion.104
  12.1 6.0 %collective-permute-start.3 = (f32[8,4,3,256]{3,2,1,0:T(4,128)}, f32[8,4,3,256]{3,2,1,0:T(4,128)}, u32[]{:S(2)}, u32[]{:S(2)}) collective-permute-start(f32[8,4,3,256]{3,2,1,0:T(4,128)} %get-tuple-element.20), channel_id=1, source_target_pairs={{0,1},{1,2},{2,3},{3,4},{4,5},{5,6},{6,7},{7,8},{8,9},{9,10},{10,1... | collective-permute-start | bytes 294920 | tf_op jit(solution)/shard_map/ppermute | solution.py:20
  18.2 1.9 collective-permute-start.4
  20.5 58.6 %all_gather.7 = f32[2,4,25,256]{2,1,0,3:T(4,128)S(1)} all-gather(f32[2,4,25,8]{2,1,0,3:T(4,128)S(1)} %copy.29), channel_id=1, replica_groups=mesh['tracer'=32,'space'=16] {'tracer'}, dimensions={3}, use_global_device_ids=true | all-gather | bytes 211200 | tf_op jit(solution)/shard_map/all_gather | solution.py:109
  79.1 1.2 fusion.102
  81.2 70.9 %all_gather.6 = f32[3,4,24,256]{2,1,0,3:T(4,128)S(1)} all-gather(f32[3,4,24,8]{2,1,0,3:T(4,128)S(1)} %copy.27), channel_id=1, replica_groups=mesh['tracer'=32,'space'=16] {'tracer'}, dimensions={3}, use_global_device_ids=true | all-gather | bytes 304128 | tf_op jit(solution)/shard_map/all_gather | solution.py:110
  152.2 1.3 fusion.101
  153.4 1.8 copy.40
  155.3 1.9 copy.38
  157.1 1.2 copy.39
  160.3 1.7 copy.31
  164.0 1.1 pad_maximum_fusion.3
  166.1 1.4 fusion.68
  167.6 1.9 fusion.62
  169.7 1.0 fusion.2
  170.6 1.0 fusion.12
  172.0 5.9 %collective-permute-start.5 = (f32[8,4,3,256]{3,2,1,0:T(4,128)S(1)}, f32[8,4,3,256]{3,2,1,0:T(4,128)S(1)}, u32[]{:S(2)}, u32[]{:S(2)}) collective-permute-start(f32[8,4,3,256]{3,2,1,0:T(4,128)S(1)} %get-tuple-element.17), channel_id=1, source_target_pairs={{0,1},{1,2},{2,3},{3,4},{4,5},{5,6},{6,7},{7,8},{8,9},{9,10},{10,1... | collective-permute-start | bytes 294920 | tf_op jit(solution)/shard_map/ppermute | solution.py:20
  177.9 1.9 collective-permute-start.6
  180.9 6.2 %collective-permute-done.6 = f32[8,4,3,256]{3,2,1,0:T(4,128)S(1)} collective-permute-done((f32[8,4,3,256]{3,2,1,0:T(4,128)S(1)}, f32[8,4,3,256]{3,2,1,0:T(4,128)S(1)}, u32[]{:S(2)}, u32[]{:S(2)}) %collective-permute-start.6) | collective-permute-done | bytes 98336 | tf_op jit(solution)/shard_map/ppermute | solution.py:22
  190.2 1.0 fusion.31
  191.2 1.2 fusion.77
  (66 shorter events, 12.3 us)
Async XLA Ops:
  0.6 19.5 %copy-start = (f32[8,4,24,256]{3,2,1,0:T(8,128)S(1)}, f32[8,4,24,256]{3,2,1,0:T(8,128)}, u32[]{:S(2)}) copy-start(f32[8,4,24,256]{3,2,1,0:T(8,128)} %param.4) | copy-start | bytes 2359300
  1.5 18.8 %copy-start.10 = (f32[4,24,8]{1,2,0:T(8,128)S(1)}, f32[4,24,8]{1,2,0:T(8,128)}, u32[]{:S(2)}) copy-start(f32[4,24,8]{1,2,0:T(8,128)} %param.5) | copy-start | bytes 9220
  1.5 18.8 %copy-start.11 = (f32[4,24,8]{1,2,0:T(8,128)S(1)}, f32[4,24,8]{1,2,0:T(8,128)}, u32[]{:S(2)}) copy-start(f32[4,24,8]{1,2,0:T(8,128)} %param.7) | copy-start | bytes 9220
  1.5 18.8 %copy-start.12 = (f32[4,24,8]{1,2,0:T(8,128)S(1)}, f32[4,24,8]{1,2,0:T(8,128)}, u32[]{:S(2)}) copy-start(f32[4,24,8]{1,2,0:T(8,128)} %param.6) | copy-start | bytes 9220
  1.6 18.7 %collective-permute-start = (f32[3,4,1,8]{2,3,1,0:T(8,128)S(1)}, f32[3,4,1,8]{2,3,1,0:T(8,128)S(1)}, u32[]{:S(2)}, u32[]{:S(2)}) collective-permute-start(f32[3,4,1,8]{2,3,1,0:T(8,128)S(1)} %get-tuple-element.27), channel_id=1, source_target_pairs={{0,1},{1,2},{2,3},{3,4},{4,5},{5,6},{6,7},{7,8},{8,9},{9,10},{10,1... | collective-permute-start | bytes 1160 | tf_op jit(solution)/shard_map/ppermute | solution.py:20
  5.8 14.5 %collective-permute-start.1 = (f32[3,4,1,8]{2,3,1,0:T(8,128)S(1)}, f32[3,4,1,8]{2,3,1,0:T(8,128)S(1)}, u32[]{:S(2)}, u32[]{:S(2)}) collective-permute-start(f32[3,4,1,8]{2,3,1,0:T(8,128)S(1)} %get-tuple-element.28), channel_id=1, source_target_pairs={{1,0},{2,1},{3,2},{4,3},{5,4},{6,5},{7,6},{8,7},{9,8},{10,9},{11,1... | collective-permute-start | bytes 1160 | tf_op jit(solution)/shard_map/ppermute | solution.py:22
  8.4 72.7 %collective-permute-start.2 = (f32[4,24,1]{1,2,0:T(1,128)S(1)}, f32[4,24,1]{1,2,0:T(1,128)S(1)}, u32[]{:S(2)}, u32[]{:S(2)}) collective-permute-start(f32[4,24,1]{1,2,0:T(1,128)S(1)} %slice.215), channel_id=1, source_target_pairs={{0,16},{16,32},{32,48},{48,64},{64,80},{80,96},{96,112},{112,128},... | collective-permute-start | bytes 1160 | tf_op jit(solution)/shard_map/ppermute | solution.py:32
  12.1 151.8 %collective-permute-start.3 = (f32[8,4,3,256]{3,2,1,0:T(4,128)}, f32[8,4,3,256]{3,2,1,0:T(4,128)}, u32[]{:S(2)}, u32[]{:S(2)}) collective-permute-start(f32[8,4,3,256]{3,2,1,0:T(4,128)} %get-tuple-element.20), channel_id=1, source_target_pairs={{0,1},{1,2},{2,3},{3,4},{4,5},{5,6},{6,7},{7,8},{8,9},{9,10},{10,1... | collective-permute-start | bytes 294920 | tf_op jit(solution)/shard_map/ppermute | solution.py:20
  18.2 145.8 %collective-permute-start.4 = (f32[8,4,3,256]{3,2,1,0:T(4,128)}, f32[8,4,3,256]{3,2,1,0:T(4,128)}, u32[]{:S(2)}, u32[]{:S(2)}) collective-permute-start(f32[8,4,3,256]{3,2,1,0:T(4,128)} %get-tuple-element.19), channel_id=1, source_target_pairs={{1,0},{2,1},{3,2},{4,3},{5,4},{6,5},{7,6},{8,7},{9,8},{10,9},{11,1... | collective-permute-start | bytes 294920 | tf_op jit(solution)/shard_map/ppermute | solution.py:22
  159.2 2.8 %copy-start.1 = (f32[1,4,24,256]{2,1,0,3:T(4,128)S(1)}, f32[1,4,24,256]{2,1,0,3:T(4,128)}, u32[]{:S(2)}) copy-start(f32[1,4,24,256]{2,1,0,3:T(4,128)} %get-tuple-element.10) | copy-start | bytes 294916
  160.1 2.8 %copy-start.6 = (f32[1,4,24,256]{3,2,1,0:T(8,128)S(1)}, f32[1,4,24,256]{3,2,1,0:T(8,128)}, u32[]{:S(2)}) copy-start(f32[1,4,24,256]{3,2,1,0:T(8,128)} %copy.40) | copy-start | bytes 294916
  160.1 2.8 %copy-start.4 = (f32[1,4,24,256]{3,2,1,0:T(8,128)S(1)}, f32[1,4,24,256]{3,2,1,0:T(8,128)}, u32[]{:S(2)}) copy-start(f32[1,4,24,256]{3,2,1,0:T(8,128)} %copy.38) | copy-start | bytes 294916
  162.3 0.6 copy-start.7
  166.1 1.5 copy-start.2
  166.1 1.5 copy-start.3
  166.1 1.5 copy-start.8
  167.6 1.9 copy-start.5
  172.0 8.9 %collective-permute-start.5 = (f32[8,4,3,256]{3,2,1,0:T(4,128)S(1)}, f32[8,4,3,256]{3,2,1,0:T(4,128)S(1)}, u32[]{:S(2)}, u32[]{:S(2)}) collective-permute-start(f32[8,4,3,256]{3,2,1,0:T(4,128)S(1)} %get-tuple-element.17), channel_id=1, source_target_pairs={{0,1},{1,2},{2,3},{3,4},{4,5},{5,6},{6,7},{7,8},{8,9},{9,10},{10,1... | collective-permute-start | bytes 294920 | tf_op jit(solution)/shard_map/ppermute | solution.py:20
  177.9 9.3 %collective-permute-start.6 = (f32[8,4,3,256]{3,2,1,0:T(4,128)S(1)}, f32[8,4,3,256]{3,2,1,0:T(4,128)S(1)}, u32[]{:S(2)}, u32[]{:S(2)}) collective-permute-start(f32[8,4,3,256]{3,2,1,0:T(4,128)S(1)} %get-tuple-element.18), channel_id=1, source_target_pairs={{1,0},{2,1},{3,2},{4,3},{5,4},{6,5},{7,6},{8,7},{9,8},{10,9},{11,1... | collective-permute-start | bytes 294920 | tf_op jit(solution)/shard_map/ppermute | solution.py:22
  187.3 0.8 copy-start.9
where the time goes:
time: 193 us; the launch traced here: 192 us
  blocking collectives  130 us (67%)
  starting transfers between devices  23.8 us (12%)
  other arithmetic  15.8 us (8%)
  local copies, waits for them, and re-layouts  15.6 us (8%)
  waiting for transfers between devices  6.6 us (3%)
    all_gather x1, blocking collectives, per_device(): lax.all_gather(jnp.stack([cy, mfy, thick]), 'tracer', axis=3, tiled=True)  70.9 us
    all_gather x1, blocking collectives, per_device(): lax.all_gather(jnp.stack([cx, mfx]), 'tracer', axis=3, tiled=True)  58.6 us
    ppermute x3, starting transfers between devices, extended(): lax.ppermute(tail, axis, [(i, (i + 1) % count) for i in range(ends)])  16.1 us
    unnamed x32, local copies, waits for them, and re-layouts  6.87 us
    ppermute x3, waiting for transfers between devices, extended(): lax.ppermute(head, axis, [((i + 1) % count, i) for i in range(ends)])  6.23 us
    ppermute x3, starting transfers between devices, extended(): lax.ppermute(head, axis, [((i + 1) % count, i) for i in range(ends)])  5.76 us
    mul x4, other arithmetic, sweep(): flux = mass_flux * face_values(padded, courant, count, axis)  4.8 us
  transfers between devices with their start and end apart: 7, of which 2 were waited for; matrix products, arithmetic and copies ran while one was open for 9% of the time, Pallas kernels for 0%

commit v1 on v0

v1 whole, which is shorter than its diff:
```python
import jax
import jax.numpy as jnp
from jax import lax
from jax.experimental import pallas as pl
from jax.experimental.pallas import tpu as pltpu
from jax.sharding import PartitionSpec as P

COURANT_SCALE = 0.025
LEV, ROWS, COLS, TR = 4, 24, 256, 8
BLOCK = 8
REACH = 3
HALO = 2 * REACH
SIDE = 4
SPAN = ROWS + 2 * SIDE
VMEM = pl.BlockSpec(memory_space=pltpu.VMEM)
PARAMS = pltpu.CompilerParams(vmem_limit_bytes=24 * 1024 * 1024)


def pack_fields(thick, wind_x, wind_y, packed):
    for f, field in enumerate((thick, wind_x, wind_y)):
        parts = []
        for l in range(LEV):
            own = field[l]
            parts += [own[:, ROWS - SIDE :], own, own[:, :SIDE]]
        packed[f] = jnp.concatenate(parts, axis=1)


def tile_rows(x):
    x = x.reshape(TR, LEV, ROWS // 8, 8, COLS // 128, 128)
    return jnp.transpose(x, (0, 1, 2, 4, 3, 5)).reshape(-1, 128)


def from_tile_rows(x):
    x = x.reshape(TR, LEV, ROWS // 8, COLS // 128, 8, 128)
    return jnp.transpose(x, (0, 1, 2, 4, 3, 5)).reshape(TR, LEV, ROWS, COLS)


def row_of_all(l, r, half):
    start = (l * (ROWS // 8) + r // 8) * (COLS // 128) * 8 + half * 8 + r % 8
    return pl.ds(start, TR, stride=LEV * ROWS * (COLS // 128))


def get_row(ref, l, r):
    return jnp.concatenate([ref[row_of_all(l, r, h), :] for h in range(2)], axis=1)


def pack_halos(tracers, low, high):
    for l in range(LEV):
        for r in range(HALO):
            low[l, r] = get_row(tracers, l, r)
            high[l, r] = get_row(tracers, l, ROWS - HALO + r)


def stencil(courant, flux, after):
    size = jnp.abs(courant)
    half = 0.5 * size
    curve = 3.0 * half * (1.0 - (2.0 / 3.0) * size)
    near = flux * (1.0 - half - curve)
    far = flux * (half - curve)
    mean = flux * (2.0 * curve)
    up = courant > 0
    far_l = jnp.where(up, far, 0.0)
    far_r = far - far_l
    mean_l = jnp.where(up, mean, 0.0)
    mean_r = mean - mean_l
    in_, out = 7.0 / 12.0, 1.0 / 12.0
    face = [
        -out * far_l,
        in_ * far_l - out * near,
        in_ * (far_l + near) - out * far_r + mean_l,
        in_ * (far_r + near) - out * far_l + mean_r,
        in_ * far_r - out * near,
        -out * far_r,
    ]
    moved = [after(w) for w in face]
    return (
        [face[0]]
        + [face[j] - moved[j - 1] for j in range(1, 6)]
        + [-moved[5]]
    )


def sweeps(
    gathered, tracers, low, high, out, thick_out, fields, mid, weights, ends, turned
):
    space = lax.axis_index("space")
    tracer = lax.axis_index("tracer")
    last_row = lax.axis_size("space") * ROWS
    for f in range(3):
        blocks = [
            gathered[c, j, f * BLOCK : (f + 1) * BLOCK, :]
            for j in range(16)
            for c in range(2)
        ]
        fields[f] = jnp.concatenate(blocks, axis=0).T

    row = lax.broadcasted_iota(jnp.int32, (SPAN, COLS), 0) + (space * ROWS - SIDE)
    col = lax.broadcasted_iota(jnp.int32, (SPAN, COLS), 1)

    def level(l, carry):
        at = pl.ds(pl.multiple_of(l * SPAN, SPAN), SPAN)
        inside = (row >= 0) & (row < last_row)
        thick = jnp.where(inside, fields[0, at, :], 1.0)
        next_row = lambda x: pltpu.roll(x, SPAN - 1, 0)
        next_col = lambda x: pltpu.roll(x, COLS - 1, 1)

        cx = jnp.where((row > 0) & (row < last_row), COURANT_SCALE * fields[1, at, :], 0.0)
        mfx = cx * jnp.where(cx > 0, pltpu.roll(thick, 1, 0), thick)
        cy = jnp.where(col > 0, COURANT_SCALE * fields[2, at, :], 0.0)
        mfy = cy * jnp.where(cy > 0, pltpu.roll(thick, 1, 1), thick)
        thin_x = next_row(mfx) - mfx
        thin_y = next_col(mfy) - mfy
        dp1 = thick - thin_x
        dp2 = dp1 - thin_y
        dp3 = dp2 - thin_x
        dp4 = dp3 - thin_y
        ends[at, :] = dp4
        r1, r2, r3, r4 = 1.0 / dp1, 1.0 / dp2, 1.0 / dp3, 1.0 / dp4

        def put(n, j, add, r_a, dp_a, r_b, dp_b):
            if j == 3:
                weights[n, j] = (add + dp_a) * r_a
                weights[n + 2, j] = (add + dp_b) * r_b
            else:
                weights[n, j] = add * r_a
                weights[n + 2, j] = add * r_b

        for j, add in enumerate(stencil(cx, mfx, next_row)):
            put(0, j, add, r1, thick, r3, dp2)
        for j, add in enumerate(stencil(cy, mfy, next_col)):
            step = j - REACH
            if step < 0:
                add = jnp.where(col >= -step, add, 0.0)
            elif step > 0:
                add = jnp.where(col < COLS - step, add, 0.0)
            put(1, j, add, r2, dp1, r4, dp3)

        def weight(n, j, r):
            return weights[n, j, r + SIDE : r + SIDE + 1, :]

        def both(cells, n, r):
            total = weight(n, 0, r) * cells[0]
            for j in range(1, 7):
                total += weight(n, j, r) * cells[j]
            result = weight(n + 1, REACH, r) * total
            for j in range(7):
                if j != REACH:
                    shift = (REACH - j) % COLS
                    result += weight(n + 1, j, r) * pltpu.roll(total, shift, 1)
            return result

        def first(r):
            if r < 0:
                return low[l, r + HALO]
            if r >= ROWS:
                return high[l, r - ROWS]
            return get_row(tracers, l, r)

        window = [first(r) for r in range(-HALO, 0)]
        for r in range(-REACH, ROWS + REACH):
            window.append(first(r + REACH))
            mid[r + REACH] = both(window, 0, r)
            window.pop(0)
        window = [mid[r] for r in range(HALO)]
        for r in range(ROWS):
            window.append(mid[r + HALO])
            done = both(window, 2, r)
            for h in range(2):
                out[row_of_all(l, r, h), :] = done[:, h * 128 : (h + 1) * 128]
            window.pop(0)
        return carry

    lax.fori_loop(0, LEV, level, 0)
    turned[...] = ends[...].T
    block = turned[pl.ds(pl.multiple_of(tracer * BLOCK, BLOCK), BLOCK), :]
    for l in range(LEV):
        start = l * SPAN + SIDE
        thick_out[l] = block[:, start : start + ROWS]


def shape(*dims):
    return jax.ShapeDtypeStruct(dims, jnp.float32)


def both_ways(up, down):
    count = lax.axis_size("space")
    route = [(i, i + 1) for i in range(count - 1)]
    back = [(b, a) for a, b in route]
    return lax.ppermute(up, "space", route), lax.ppermute(down, "space", back)


def per_device(tracers, thickness, wind_x, wind_y):
    count = lax.axis_size("tracer")
    turn = lambda x: jnp.transpose(x, (0, 2, 1))
    packed = pl.pallas_call(
        pack_fields,
        out_shape=shape(3, BLOCK, LEV * SPAN),
        in_specs=[VMEM] * 3,
        out_specs=VMEM,
        compiler_params=PARAMS,
    )(turn(thickness), turn(wind_x), turn(wind_y))
    below, above = both_ways(packed, packed)

    flat = tile_rows(tracers)
    low, high = pl.pallas_call(
        pack_halos,
        out_shape=[shape(LEV, HALO, TR, COLS)] * 2,
        in_specs=[VMEM],
        out_specs=[VMEM] * 2,
        compiler_params=PARAMS,
    )(flat)
    from_below, from_above = both_ways(high, low)

    place = lax.broadcasted_iota(jnp.int32, packed.shape, 2) % SPAN
    packed = jnp.where(
        place < SIDE, below, jnp.where(place >= SIDE + ROWS, above, packed)
    ).reshape(3 * BLOCK, LEV * SPAN)
    same_core = [list(range(c, count, 2)) for c in range(2)]
    same_chip = [[i, i + 1] for i in range(0, count, 2)]
    copies = jnp.broadcast_to(packed, (count // 2,) + packed.shape)
    gathered = lax.all_to_all(copies, "tracer", 0, 0, axis_index_groups=same_core)
    gathered = lax.all_gather(gathered, "tracer", axis_index_groups=same_chip)

    values, thick = pl.pallas_call(
        sweeps,
        out_shape=[shape(TR * LEV * ROWS * 2, 128), shape(LEV, BLOCK, ROWS)],
        in_specs=[VMEM] * 4,
        out_specs=[VMEM] * 2,
        scratch_shapes=[
            pltpu.VMEM((3, LEV * SPAN, COLS), jnp.float32),
            pltpu.VMEM((ROWS + HALO, TR, COLS), jnp.float32),
            pltpu.VMEM((4, 7, SPAN, COLS), jnp.float32),
            pltpu.VMEM((LEV * SPAN, COLS), jnp.float32),
            pltpu.VMEM((COLS, LEV * SPAN), jnp.float32),
        ],
        compiler_params=PARAMS,
    )(gathered, flat, from_below, from_above)
    return from_tile_rows(values), turn(thick)


def solution(mesh):
    in_specs = (
        P("tracer", None, "space", None),
        P(None, "space", "tracer"),
        P(None, "space", "tracer"),
        P(None, "space", "tracer"),
    )
    out_specs = (P("tracer", None, "space", None), P(None, "space", "tracer"))
    return jax.shard_map(
        per_device, mesh=mesh, in_specs=in_specs, out_specs=out_specs, check_vma=False
    )
```

time: 193 us -> 53 us (0.27)
  the two profiles are of different devices: /device:TPU:30 before, /device:TPU:65 now
where the time goes in v1:
time: 53 us; the launch traced here: 52.4 us
  starting transfers between devices  28.2 us (53%)
  waiting for transfers between devices  8.85 us (17%)
  Pallas kernels  5.42 us (10%)
  blocking collectives  5.29 us (10%)
  local copies, waits for them, and re-layouts  3.97 us (7%)
  between operations  0.73 us (1%)
    all_to_all x1, starting transfers between devices, per_device(): lax.all_to_all(copies, 'tracer', 0, 0, axis_index_groups=same_core)  15.4 us
    ppermute x4, starting transfers between devices, both_ways(): return (lax.ppermute(up, 'space', route), lax.ppermute(down, 'space', back))  12.8 us
    all_gather x1, blocking collectives, per_device(): gathered = lax.all_gather(gathered, 'tracer', axis_index_groups=same_chip)  5.29 us
    pallas_call x1, Pallas kernels, per_device(): pl.pallas_call(sweeps, out_shape=[shape(TR * LEV * ROWS * 2, 128), shape(...  5.09 us
    ppermute x4, waiting for transfers between devices, both_ways(): return (lax.ppermute(up, 'space', route), lax.ppermute(down, 'space', back))  4.6 us
    all_to_all x1, waiting for transfers between devices, per_device(): lax.all_to_all(copies, 'tracer', 0, 0, axis_index_groups=same_core)  4.25 us
    unnamed x10, local copies, waits for them, and re-layouts  3.28 us
  transfers between devices with their start and end apart: 5, of which 2 were waited for; matrix products, arithmetic and copies ran while one was open for 0% of the time, Pallas kernels for 0%

profile of v1, /device:TPU:65, one launch (start us, length us, event | category | flops | bytes accessed | tf_op | source)
XLA Modules:
  0.0 52.4 jit_solution(4775266862074281107)
XLA Ops:
  0.6 0.0 copy-start.2
  0.6 0.7 %copy-done.2 = f32[4,24,8]{1,2,0:T(8,128)S(1)} copy-done((f32[4,24,8]{1,2,0:T(8,128)S(1)}, f32[4,24,8]{1,2,0:T(8,128)}, u32[]{:S(2)}) %copy-start.2) | copy-done | bytes 3096
  1.3 0.0 copy-start.3
  1.4 0.7 %copy-done.3 = f32[4,24,8]{1,2,0:T(8,128)S(1)} copy-done((f32[4,24,8]{1,2,0:T(8,128)S(1)}, f32[4,24,8]{1,2,0:T(8,128)}, u32[]{:S(2)}) %copy-start.3) | copy-done | bytes 3096
  2.1 0.0 copy-start.4
  2.1 0.7 %copy-done.4 = f32[4,24,8]{1,2,0:T(8,128)S(1)} copy-done((f32[4,24,8]{1,2,0:T(8,128)S(1)}, f32[4,24,8]{1,2,0:T(8,128)}, u32[]{:S(2)}) %copy-start.4) | copy-done | bytes 3096
  2.8 0.1 shard_map.59
  2.9 3.5 %collective-permute-start.1 = (f32[3,8,128]{2,1,0:T(8,128)S(1)}, f32[3,8,128]{2,1,0:T(8,128)S(1)}, u32[]{:S(2)}, u32[]{:S(2)}) collective-permute-start(f32[3,8,128]{2,1,0:T(8,128)S(1)} %shard_map.59), channel_id=1, source_target_pairs={{1,0},{2,1},{3,2},{4,3},{5,4},{6,5},{7,6},{8,7},{9,8},{10,9},{11,1... | collective-permute-start | bytes 36872 | tf_op jit(solution)/shard_map/ppermute | solution.py:189
  6.4 1.9 %collective-permute-start = (f32[3,8,128]{2,1,0:T(8,128)S(1)}, f32[3,8,128]{2,1,0:T(8,128)S(1)}, u32[]{:S(2)}, u32[]{:S(2)}) collective-permute-start(f32[3,8,128]{2,1,0:T(8,128)S(1)} %shard_map.59), channel_id=1, source_target_pairs={{0,1},{1,2},{2,3},{3,4},{4,5},{5,6},{6,7},{7,8},{8,9},{9,10},{10,1... | collective-permute-start | bytes 36872 | tf_op jit(solution)/shard_map/ppermute | solution.py:189
  8.3 0.0 collective-permute-done.1
  8.3 4.6 %collective-permute-done = f32[3,8,128]{2,1,0:T(8,128)S(1)} collective-permute-done((f32[3,8,128]{2,1,0:T(8,128)S(1)}, f32[3,8,128]{2,1,0:T(8,128)S(1)}, u32[]{:S(2)}, u32[]{:S(2)}) %collective-permute-start) | collective-permute-done | bytes 12320 | tf_op jit(solution)/shard_map/ppermute | solution.py:189
  12.9 0.7 %broadcast_in_dim.3 = f32[16,24,128]{2,1,0:T(8,128)} broadcast(f32[24,128]{1,0:T(8,128)S(1)} %select_bitcast_fusion), dimensions={1,2} | broadcast | bytes 208896 | tf_op jit(solution)/shard_map/broadcast_in_dim | solution.py:220
  13.6 15.4 %all-to-all-start = ((f32[16,24,128]{2,1,0:T(8,128)}), f32[16,24,128]{2,1,0:T(8,128)S(1)}, u32[]{:S(2)}, u32[]{:S(2)}) async-start(f32[16,24,128]{2,1,0:T(8,128)} %broadcast_in_dim.3), calls=%async_computation | async-start | bytes 393216 | tf_op jit(solution)/shard_map/all_to_all | solution.py:221
  29.0 0.0 copy-start
  29.0 1.1 %copy-done = f32[8,4,24,256]{3,2,1,0:T(8,128)S(1)} copy-done((f32[8,4,24,256]{3,2,1,0:T(8,128)S(1)}, f32[8,4,24,256]{3,2,1,0:T(8,128)}, u32[]{:S(2)}) %copy-start) | copy-done | bytes 786456
  30.1 0.2 shard_map.60
  30.4 1.9 %collective-permute-start.2 = (f32[4,6,8,256]{3,2,1,0:T(8,128)S(1)}, f32[4,6,8,256]{3,2,1,0:T(8,128)S(1)}, u32[]{:S(2)}, u32[]{:S(2)}) collective-permute-start(f32[4,6,8,256]{3,2,1,0:T(8,128)S(1)} %get-tuple-element.6), channel_id=1, source_target_pairs={{0,1},{1,2},{2,3},{3,4},{4,5},{5,6},{6,7},{7,8},{8,9},{9,10},{10,1... | collective-permute-start | bytes 589832 | tf_op jit(solution)/shard_map/ppermute | solution.py:189
  32.3 5.5 %collective-permute-start.3 = (f32[4,6,8,256]{3,2,1,0:T(8,128)S(1)}, f32[4,6,8,256]{3,2,1,0:T(8,128)S(1)}, u32[]{:S(2)}, u32[]{:S(2)}) collective-permute-start(f32[4,6,8,256]{3,2,1,0:T(8,128)S(1)} %get-tuple-element.7), channel_id=1, source_target_pairs={{1,0},{2,1},{3,2},{4,3},{5,4},{6,5},{7,6},{8,7},{9,8},{10,9},{11,1... | collective-permute-start | bytes 589832 | tf_op jit(solution)/shard_map/ppermute | solution.py:189
  37.8 4.3 %all-to-all-done = f32[16,24,128]{2,1,0:T(8,128)S(1)} async-done(((f32[16,24,128]{2,1,0:T(8,128)}), f32[16,24,128]{2,1,0:T(8,128)S(1)}, u32[]{:S(2)}, u32[]{:S(2)}) %all-to-all-start) | async-done | bytes 196640 | tf_op jit(solution)/shard_map/all_to_all | solution.py:221
  42.0 5.3 %all-gather = f32[32,24,128]{2,1,0:T(8,128)S(1)} all-gather(f32[16,24,128]{2,1,0:T(8,128)S(1)} %all-to-all-done), channel_id=2, replica_groups={{0,16},{32,48},{64,80},{96,112},{128,144},{160,176},{192,208},{224,240}..., dimensions={0}, use_global_device_ids=true | all-gather | bytes 589824 | tf_op jit(solution)/shard_map/all_gather | solution.py:222
  47.3 0.0 collective-permute-done.2.low
  47.3 0.0 collective-permute-done.3.high
  47.3 0.0 copy-done.1
  47.3 5.1 %shard_map.61 = (f32[1536,128]{1,0:T(8,128)}, f32[4,8,24]{2,1,0:T(8,128)}) custom-call(f32[2,16,24,128]{3,2,1,0:T(8,128)S(1)} %bitcast.19, f32[1536,128]{1,0:T(8,128)S(1)} %bitcast.18, f32[4,6,8,256]{3,2,1,0:T(8,128)S(1)} %collective-permute-done.2.low, f32[4,6,8,256]{3,2,1,0:T(8,128)S(1)} %collective-permute-done.3.high), custom_call_target="tpu_custom_call" | custom-call | tf_op jit(solution)/shard_map/pallas_call | solution.py:224
  (4 shorter events, 0.0 us)
Async XLA Ops:
  0.6 0.7 %copy-start.2 = (f32[4,24,8]{1,2,0:T(8,128)S(1)}, f32[4,24,8]{1,2,0:T(8,128)}, u32[]{:S(2)}) copy-start(f32[4,24,8]{1,2,0:T(8,128)} %param.5) | copy-start | bytes 9220
  1.3 0.7 %copy-start.3 = (f32[4,24,8]{1,2,0:T(8,128)S(1)}, f32[4,24,8]{1,2,0:T(8,128)}, u32[]{:S(2)}) copy-start(f32[4,24,8]{1,2,0:T(8,128)} %param.6) | copy-start | bytes 9220
  2.1 0.7 %copy-start.4 = (f32[4,24,8]{1,2,0:T(8,128)S(1)}, f32[4,24,8]{1,2,0:T(8,128)}, u32[]{:S(2)}) copy-start(f32[4,24,8]{1,2,0:T(8,128)} %param.7) | copy-start | bytes 9220
  2.9 5.4 %collective-permute-start.1 = (f32[3,8,128]{2,1,0:T(8,128)S(1)}, f32[3,8,128]{2,1,0:T(8,128)S(1)}, u32[]{:S(2)}, u32[]{:S(2)}) collective-permute-start(f32[3,8,128]{2,1,0:T(8,128)S(1)} %shard_map.59), channel_id=1, source_target_pairs={{1,0},{2,1},{3,2},{4,3},{5,4},{6,5},{7,6},{8,7},{9,8},{10,9},{11,1... | collective-permute-start | bytes 36872 | tf_op jit(solution)/shard_map/ppermute | solution.py:189
  6.4 6.5 %collective-permute-start = (f32[3,8,128]{2,1,0:T(8,128)S(1)}, f32[3,8,128]{2,1,0:T(8,128)S(1)}, u32[]{:S(2)}, u32[]{:S(2)}) collective-permute-start(f32[3,8,128]{2,1,0:T(8,128)S(1)} %shard_map.59), channel_id=1, source_target_pairs={{0,1},{1,2},{2,3},{3,4},{4,5},{5,6},{6,7},{7,8},{8,9},{9,10},{10,1... | collective-permute-start | bytes 36872 | tf_op jit(solution)/shard_map/ppermute | solution.py:189
  13.6 28.4 %all-to-all-start = ((f32[16,24,128]{2,1,0:T(8,128)}), f32[16,24,128]{2,1,0:T(8,128)S(1)}, u32[]{:S(2)}, u32[]{:S(2)}) async-start(f32[16,24,128]{2,1,0:T(8,128)} %broadcast_in_dim.3), calls=%async_computation | async-start | bytes 393216 | tf_op jit(solution)/shard_map/all_to_all | solution.py:221
  29.0 1.1 %copy-start = (f32[8,4,24,256]{3,2,1,0:T(8,128)S(1)}, f32[8,4,24,256]{3,2,1,0:T(8,128)}, u32[]{:S(2)}) copy-start(f32[8,4,24,256]{3,2,1,0:T(8,128)} %param.4) | copy-start | bytes 2359300
  30.1 17.2 %copy-start.1 = (f32[8,4,24,256]{3,2,1,0:T(8,128)S(1)}, f32[8,4,24,256]{3,2,1,0:T(8,128)}, u32[]{:S(2)}) copy-start(f32[8,4,24,256]{3,2,1,0:T(8,128)} %param.4) | copy-start | bytes 2359300
  30.4 17.0 %collective-permute-start.2 = (f32[4,6,8,256]{3,2,1,0:T(8,128)S(1)}, f32[4,6,8,256]{3,2,1,0:T(8,128)S(1)}, u32[]{:S(2)}, u32[]{:S(2)}) collective-permute-start(f32[4,6,8,256]{3,2,1,0:T(8,128)S(1)} %get-tuple-element.6), channel_id=1, source_target_pairs={{0,1},{1,2},{2,3},{3,4},{4,5},{5,6},{6,7},{7,8},{8,9},{9,10},{10,1... | collective-permute-start | bytes 589832 | tf_op jit(solution)/shard_map/ppermute | solution.py:189
  32.3 15.0 %collective-permute-start.3 = (f32[4,6,8,256]{3,2,1,0:T(8,128)S(1)}, f32[4,6,8,256]{3,2,1,0:T(8,128)S(1)}, u32[]{:S(2)}, u32[]{:S(2)}) collective-permute-start(f32[4,6,8,256]{3,2,1,0:T(8,128)S(1)} %get-tuple-element.7), channel_id=1, source_target_pairs={{1,0},{2,1},{3,2},{4,3},{5,4},{6,5},{7,6},{8,7},{9,8},{10,9},{11,1... | collective-permute-start | bytes 589832 | tf_op jit(solution)/shard_map/ppermute | solution.py:189

commit v2 on v1

--- a/solution.py
+++ b/solution.py
@@ -16,13 +16,40 @@
 PARAMS = pltpu.CompilerParams(vmem_limit_bytes=24 * 1024 * 1024)
 
 
-def pack_fields(thick, wind_x, wind_y, packed):
-    for f, field in enumerate((thick, wind_x, wind_y)):
+def pack_fields(thick, wind_x, wind_y, packed, held, arrived):
+    copies = [
+        pltpu.make_async_copy(field, held.at[f], arrived.at[f])
+        for f, field in enumerate((thick, wind_x, wind_y))
+    ]
+    for copy in copies:
+        copy.start()
+    for f, copy in enumerate(copies):
+        copy.wait()
         parts = []
         for l in range(LEV):
-            own = field[l]
+            own = held[f, l]
             parts += [own[:, ROWS - SIDE :], own, own[:, :SIDE]]
         packed[f] = jnp.concatenate(parts, axis=1)
+
+
+def spread(pair, copies):
+    core = lax.axis_index("tracer") % 2
+    place = lax.broadcasted_iota(jnp.int32, (BLOCK, LEV * SPAN), 1) % SPAN
+    half = copies.shape[0] // 2
+    for f in range(3):
+        here = slice(f * BLOCK, (f + 1) * BLOCK)
+        first, second = pair[0, f], pair[1, f]
+        own = jnp.where(core == 0, first, second)
+        last_rows = jnp.where(place < SIDE, first, pltpu.roll(second, SIDE, 1))
+        first_rows = jnp.where(
+            place >= SPAN - SIDE, second, pltpu.roll(first, LEV * SPAN - SIDE, 1)
+        )
+        beside = jnp.where(core == 0, last_rows, first_rows)
+        to_first = jnp.where(core == 0, own, beside)
+        to_second = jnp.where(core == 0, beside, own)
+        for i in range(half):
+            copies[i, here, :] = to_first
+            copies[half + i, here, :] = to_second
 
 
 def tile_rows(x):
@@ -44,11 +71,14 @@
     return jnp.concatenate([ref[row_of_all(l, r, h), :] for h in range(2)], axis=1)
 
 
-def pack_halos(tracers, low, high):
+def pack_halos(tracers, once, twice):
+    odd = lax.axis_index("space") % 2 == 1
     for l in range(LEV):
         for r in range(HALO):
-            low[l, r] = get_row(tracers, l, r)
-            high[l, r] = get_row(tracers, l, ROWS - HALO + r)
+            low = get_row(tracers, l, r)
+            high = get_row(tracers, l, ROWS - HALO + r)
+            once[l, r] = jnp.where(odd, low, high)
+            twice[l, r] = jnp.where(odd, high, low)
 
 
 def stencil(courant, flux, after):
@@ -81,17 +111,30 @@
 
 
 def sweeps(
-    gathered, tracers, low, high, out, thick_out, fields, mid, weights, ends, turned
+    gathered, tracers, once, twice, out, thick_out, fields, mid, weights, ends, turned
 ):
     space = lax.axis_index("space")
     tracer = lax.axis_index("tracer")
     last_row = lax.axis_size("space") * ROWS
+    odd = space % 2 == 1
+    half = gathered.shape[1] // 2
+    place = lax.broadcasted_iota(jnp.int32, (BLOCK, LEV * SPAN), 1) % SPAN
     for f in range(3):
-        blocks = [
-            gathered[c, j, f * BLOCK : (f + 1) * BLOCK, :]
-            for j in range(16)
-            for c in range(2)
-        ]
+        here = slice(f * BLOCK, (f + 1) * BLOCK)
+        blocks = []
+        for j in range(half):
+            before = gathered[1, j, here, :]
+            after = gathered[0, half + j, here, :]
+            for own, below, above in (
+                (gathered[0, j, here, :], before, pltpu.roll(after, SIDE, 1)),
+                (
+                    gathered[1, half + j, here, :],
+                    pltpu.roll(before, LEV * SPAN - SIDE, 1),
+                    after,
+                ),
+            ):
+                own = jnp.where(place < SIDE, below, own)
+                blocks.append(jnp.where(place >= SPAN - SIDE, above, own))
         fields[f] = jnp.concatenate(blocks, axis=0).T
 
     row = lax.broadcasted_iota(jnp.int32, (SPAN, COLS), 0) + (space * ROWS - SIDE)
@@ -106,7 +149,7 @@
 
         cx = jnp.where((row > 0) & (row < last_row), COURANT_SCALE * fields[1, at, :], 0.0)
         mfx = cx * jnp.where(cx > 0, pltpu.roll(thick, 1, 0), thick)
-        cy = jnp.where(col > 0, COURANT_SCALE * fields[2, at, :], 0.0)
+        cy = jnp.where(inside & (col > 0), COURANT_SCALE * fields[2, at, :], 0.0)
         mfy = cy * jnp.where(cy > 0, pltpu.roll(thick, 1, 1), thick)
         thin_x = next_row(mfx) - mfx
         thin_y = next_col(mfy) - mfy
@@ -151,9 +194,9 @@
 
         def first(r):
             if r < 0:
-                return low[l, r + HALO]
+                return jnp.where(odd, once[l, r + HALO], twice[l, r + HALO])
             if r >= ROWS:
-                return high[l, r - ROWS]
+                return jnp.where(odd, twice[l, r - ROWS], once[l, r - ROWS])
             return get_row(tracers, l, r)
 
         window = [first(r) for r in range(-HALO, 0)]
@@ -182,44 +225,56 @@
     return jax.ShapeDtypeStruct(dims, jnp.float32)
 
 
-def both_ways(up, down):
+def swap(block, start):
     count = lax.axis_size("space")
-    route = [(i, i + 1) for i in range(count - 1)]
-    back = [(b, a) for a, b in route]
-    return lax.ppermute(up, "space", route), lax.ppermute(down, "space", back)
+    pairs = [(i, i + 1) for i in range(start, count - 1, 2)]
+    return lax.ppermute(block, "space", pairs + [(b, a) for a, b in pairs])
 
 
 def per_device(tracers, thickness, wind_x, wind_y):
-    count = lax.axis_size("tracer")
+    count, steps = lax.axis_size("tracer"), lax.axis_size("space")
     turn = lambda x: jnp.transpose(x, (0, 2, 1))
     packed = pl.pallas_call(
         pack_fields,
         out_shape=shape(3, BLOCK, LEV * SPAN),
-        in_specs=[VMEM] * 3,
+        in_specs=[pl.BlockSpec(memory_space=pl.ANY)] * 3,
+        out_specs=VMEM,
+        scratch_shapes=[
+            pltpu.VMEM((3, LEV, BLOCK, ROWS), jnp.float32),
+            pltpu.SemaphoreType.DMA((3,)),
+        ],
+    )(turn(thickness), turn(wind_x), turn(wind_y))
+    same_chip = [[i, i + 1] for i in range(0, count, 2)]
+    pair = lax.all_gather(packed, "tracer", axis_index_groups=same_chip)
+    copies = pl.pallas_call(
+        spread,
+        out_shape=shape(count, 3 * BLOCK, LEV * SPAN),
+        in_specs=[VMEM],
         out_specs=VMEM,
         compiler_params=PARAMS,
-    )(turn(thickness), turn(wind_x), turn(wind_y))
-    below, above = both_ways(packed, packed)
+    )(pair)
+    members = [
+        [
+            (2 * j + core) * steps + (place + core) % steps
+            for core in range(2)
+            for j in range(count // 2)
+        ]
+        for place in range(steps)
+    ]
+    gathered = lax.all_to_all(
+        copies, ("tracer", "space"), 0, 0, axis_index_groups=members
+    )
+    gathered = lax.all_gather(gathered, "tracer", axis_index_groups=same_chip)
 
     flat = tile_rows(tracers)
-    low, high = pl.pallas_call(
+    once, twice = pl.pallas_call(
         pack_halos,
         out_shape=[shape(LEV, HALO, TR, COLS)] * 2,
         in_specs=[VMEM],
         out_specs=[VMEM] * 2,
         compiler_params=PARAMS,
     )(flat)
-    from_below, from_above = both_ways(high, low)
-
-    place = lax.broadcasted_iota(jnp.int32, packed.shape, 2) % SPAN
-    packed = jnp.where(
-        place < SIDE, below, jnp.where(place >= SIDE + ROWS, above, packed)
-    ).reshape(3 * BLOCK, LEV * SPAN)
-    same_core = [list(range(c, count, 2)) for c in range(2)]
-    same_chip = [[i, i + 1] for i in range(0, count, 2)]
-    copies = jnp.broadcast_to(packed, (count // 2,) + packed.shape)
-    gathered = lax.all_to_all(copies, "tracer", 0, 0, axis_index_groups=same_core)
-    gathered = lax.all_gather(gathered, "tracer", axis_index_groups=same_chip)
+    once, twice = swap(once, 0), swap(twice, 1)
 
     values, thick = pl.pallas_call(
         sweeps,
@@ -234,7 +289,7 @@
             pltpu.VMEM((COLS, LEV * SPAN), jnp.float32),
         ],
         compiler_params=PARAMS,
-    )(gathered, flat, from_below, from_above)
+    )(gathered, flat, once, twice)
     return from_tile_rows(values), turn(thick)
 
 

time: 53 us -> 50.2 us (0.947)
  the two profiles are of different devices: /device:TPU:65 before, /device:TPU:1 now
where the time goes in v2:
time: 50.2 us; the launch traced here: 49.9 us
  starting transfers between devices  18.4 us (37%)
  waiting for transfers between devices  11.9 us (24%)
  blocking collectives  10.9 us (22%)
  Pallas kernels  7.94 us (16%)
  between operations  0.69 us (1%)
    all_to_all x1, starting transfers between devices, per_device(): lax.all_to_all(copies, ('tracer', 'space'), 0, 0, axis_index_groups=members)  15.8 us
    all_to_all x1, waiting for transfers between devices, per_device(): lax.all_to_all(copies, ('tracer', 'space'), 0, 0, axis_index_groups=members)  11.9 us
    all_gather x1, blocking collectives, per_device(): pair = lax.all_gather(packed, 'tracer', axis_index_groups=same_chip)  8.58 us
    pallas_call x1, Pallas kernels, per_device(): pl.pallas_call(sweeps, out_shape=[shape(TR * LEV * ROWS * 2, 128), shape(...  5.22 us
    ppermute x2, starting transfers between devices, swap(): return lax.ppermute(block, 'space', pairs + [(b, a) for a, b in pairs])  2.59 us
    all_gather x1, blocking collectives, per_device(): gathered = lax.all_gather(gathered, 'tracer', axis_index_groups=same_chip)  2.36 us
    pallas_call x1, Pallas kernels, per_device(): pl.pallas_call(pack_fields, out_shape=shape(3, BLOCK, LEV * SPAN), in_spe...  1.66 us
  transfers between devices with their start and end apart: 3, of which 1 were waited for; matrix products, arithmetic and copies ran while one was open for 0% of the time, Pallas kernels for 0%

profile of v2, /device:TPU:1, one launch (start us, length us, event | category | flops | bytes accessed | tf_op | source)
XLA Modules:
  0.0 49.9 jit_solution(3518865820780763958)
XLA Ops:
  0.6 0.0 copy-start
  0.6 1.7 %shard_map.59 = f32[3,8,128]{2,1,0:T(8,128)} custom-call(f32[4,8,24]{2,1,0:T(8,128)} %bitcast.20, f32[4,8,24]{2,1,0:T(8,128)} %bitcast.21, f32[4,8,24]{2,1,0:T(8,128)} %bitcast.22), custom_call_target="tpu_custom_call" | custom-call | tf_op jit(solution)/shard_map/pallas_call | solution.py:237
  2.3 8.6 %all-gather = f32[6,8,128]{2,1,0:T(8,128)S(1)} all-gather(f32[3,8,128]{2,1,0:T(8,128)} %shard_map.59), channel_id=2, replica_groups={{0,16},{32,48},{64,80},{96,112},{128,144},{160,176},{192,208},{224,240}..., dimensions={0}, use_global_device_ids=true | all-gather | bytes 36864 | tf_op jit(solution)/shard_map/all_gather | solution.py:248
  10.9 0.8 %shard_map.60 = f32[32,24,128]{2,1,0:T(8,128)} custom-call(f32[2,3,8,128]{3,2,1,0:T(8,128)S(1)} %bitcast.19), custom_call_target="tpu_custom_call" | custom-call | tf_op jit(solution)/shard_map/pallas_call | solution.py:249
  11.7 15.8 %all-to-all-start = ((f32[32,24,128]{2,1,0:T(8,128)}), f32[32,24,128]{2,1,0:T(8,128)S(1)}, u32[]{:S(2)}, u32[]{:S(2)}) async-start(f32[32,24,128]{2,1,0:T(8,128)} %shard_map.60), calls=%async_computation | async-start | bytes 786432 | tf_op jit(solution)/shard_map/all_to_all | solution.py:264
  27.5 0.0 copy-done
  27.5 0.2 shard_map.61
  27.7 1.9 %collective-permute-start = (f32[4,6,8,256]{3,2,1,0:T(8,128)S(1)}, f32[4,6,8,256]{3,2,1,0:T(8,128)S(1)}, u32[]{:S(2)}, u32[]{:S(2)}) collective-permute-start(f32[4,6,8,256]{3,2,1,0:T(8,128)S(1)} %get-tuple-element.6), channel_id=1, source_target_pairs={{0,1},{2,3},{4,5},{6,7},{8,9},{10,11},{12,13},{14,15},{1,0},{3,2},... | collective-permute-start | bytes 589832 | tf_op jit(solution)/shard_map/ppermute | solution.py:231
  29.7 0.7 %collective-permute-start.1 = (f32[4,6,8,256]{3,2,1,0:T(8,128)S(1)}, f32[4,6,8,256]{3,2,1,0:T(8,128)S(1)}, u32[]{:S(2)}, u32[]{:S(2)}) collective-permute-start(f32[4,6,8,256]{3,2,1,0:T(8,128)S(1)} %get-tuple-element.7), channel_id=1, source_target_pairs={{1,2},{3,4},{5,6},{7,8},{9,10},{11,12},{13,14},{2,1},{4,3},{6,5},{... | collective-permute-start | bytes 589832 | tf_op jit(solution)/shard_map/ppermute | solution.py:231
  30.3 11.9 %all-to-all-done = f32[32,24,128]{2,1,0:T(8,128)S(1)} async-done(((f32[32,24,128]{2,1,0:T(8,128)}), f32[32,24,128]{2,1,0:T(8,128)S(1)}, u32[]{:S(2)}, u32[]{:S(2)}) %all-to-all-start) | async-done | bytes 393248 | tf_op jit(solution)/shard_map/all_to_all | solution.py:264
  42.3 2.4 %all-gather.1 = f32[64,24,128]{2,1,0:T(8,128)S(1)} all-gather(f32[32,24,128]{2,1,0:T(8,128)S(1)} %all-to-all-done), channel_id=3, replica_groups={{0,16},{32,48},{64,80},{96,112},{128,144},{160,176},{192,208},{224,240}..., dimensions={0}, use_global_device_ids=true | all-gather | bytes 1179648 | tf_op jit(solution)/shard_map/all_gather | solution.py:267
  44.6 0.0 collective-permute-done.once
  44.6 0.0 collective-permute-done.1.twice
  44.7 5.2 %shard_map.62 = (f32[1536,128]{1,0:T(8,128)}, f32[4,8,24]{2,1,0:T(8,128)}) custom-call(f32[2,32,24,128]{3,2,1,0:T(8,128)S(1)} %bitcast.18, f32[1536,128]{1,0:T(8,128)S(1)} %bitcast.17, f32[4,6,8,256]{3,2,1,0:T(8,128)S(1)} %collective-permute-done.once, f32[4,6,8,256]{3,2,1,0:T(8,128)S(1)} %collective-permute-done.1.twice), custom_call_target="tpu_custom_call" | custom-call | tf_op jit(solution)/shard_map/pallas_call | solution.py:279
Async XLA Ops:
  0.6 26.9 %copy-start = (f32[8,4,24,256]{3,2,1,0:T(8,128)S(1)}, f32[8,4,24,256]{3,2,1,0:T(8,128)}, u32[]{:S(2)}) copy-start(f32[8,4,24,256]{3,2,1,0:T(8,128)} %param.4) | copy-start | bytes 2359300
  11.7 30.6 %all-to-all-start = ((f32[32,24,128]{2,1,0:T(8,128)}), f32[32,24,128]{2,1,0:T(8,128)S(1)}, u32[]{:S(2)}, u32[]{:S(2)}) async-start(f32[32,24,128]{2,1,0:T(8,128)} %shard_map.60), calls=%async_computation | async-start | bytes 786432 | tf_op jit(solution)/shard_map/all_to_all | solution.py:264
  27.7 16.9 %collective-permute-start = (f32[4,6,8,256]{3,2,1,0:T(8,128)S(1)}, f32[4,6,8,256]{3,2,1,0:T(8,128)S(1)}, u32[]{:S(2)}, u32[]{:S(2)}) collective-permute-start(f32[4,6,8,256]{3,2,1,0:T(8,128)S(1)} %get-tuple-element.6), channel_id=1, source_target_pairs={{0,1},{2,3},{4,5},{6,7},{8,9},{10,11},{12,13},{14,15},{1,0},{3,2},... | collective-permute-start | bytes 589832 | tf_op jit(solution)/shard_map/ppermute | solution.py:231
  29.7 15.0 %collective-permute-start.1 = (f32[4,6,8,256]{3,2,1,0:T(8,128)S(1)}, f32[4,6,8,256]{3,2,1,0:T(8,128)S(1)}, u32[]{:S(2)}, u32[]{:S(2)}) collective-permute-start(f32[4,6,8,256]{3,2,1,0:T(8,128)S(1)} %get-tuple-element.7), channel_id=1, source_target_pairs={{1,2},{3,4},{5,6},{7,8},{9,10},{11,12},{13,14},{2,1},{4,3},{6,5},{... | collective-permute-start | bytes 589832 | tf_op jit(solution)/shard_map/ppermute | solution.py:231

commit v3 on v2

--- a/solution.py
+++ b/solution.py
@@ -6,7 +6,10 @@
 from jax.sharding import PartitionSpec as P
 
 COURANT_SCALE = 0.025
+SUBSTEPS = 2
 LEV, ROWS, COLS, TR = 4, 24, 256, 8
+HALVES = COLS // 128
+TOGETHER = 2
 BLOCK = 8
 REACH = 3
 HALO = 2 * REACH
@@ -53,32 +56,33 @@
 
 
 def tile_rows(x):
-    x = x.reshape(TR, LEV, ROWS // 8, 8, COLS // 128, 128)
+    x = x.reshape(TR, LEV, ROWS // 8, 8, HALVES, 128)
     return jnp.transpose(x, (0, 1, 2, 4, 3, 5)).reshape(-1, 128)
 
 
 def from_tile_rows(x):
-    x = x.reshape(TR, LEV, ROWS // 8, COLS // 128, 8, 128)
+    x = x.reshape(TR, LEV, ROWS // 8, HALVES, 8, 128)
     return jnp.transpose(x, (0, 1, 2, 4, 3, 5)).reshape(TR, LEV, ROWS, COLS)
 
 
-def row_of_all(l, r, half):
-    start = (l * (ROWS // 8) + r // 8) * (COLS // 128) * 8 + half * 8 + r % 8
-    return pl.ds(start, TR, stride=LEV * ROWS * (COLS // 128))
-
-
-def get_row(ref, l, r):
-    return jnp.concatenate([ref[row_of_all(l, r, h), :] for h in range(2)], axis=1)
+def tile_of(t, l, tile, half):
+    start = (((t * LEV + l) * (ROWS // 8) + tile) * HALVES + half) * 8
+    return pl.ds(pl.multiple_of(start, 8), 8)
+
+
+def halo_of(t, half):
+    return pl.ds((t * HALVES + half) * HALO, HALO)
 
 
 def pack_halos(tracers, once, twice):
     odd = lax.axis_index("space") % 2 == 1
     for l in range(LEV):
-        for r in range(HALO):
-            low = get_row(tracers, l, r)
-            high = get_row(tracers, l, ROWS - HALO + r)
-            once[l, r] = jnp.where(odd, low, high)
-            twice[l, r] = jnp.where(odd, high, low)
+        for t in range(TR):
+            for h in range(HALVES):
+                low = tracers[tile_of(t, l, 0, h), :][:HALO]
+                high = tracers[tile_of(t, l, ROWS // 8 - 1, h), :][8 - HALO :]
+                once[l, halo_of(t, h), :] = jnp.where(odd, low, high)
+                twice[l, halo_of(t, h), :] = jnp.where(odd, high, low)
 
 
 def stencil(courant, flux, after):
@@ -111,7 +115,21 @@
 
 
 def sweeps(
-    gathered, tracers, once, twice, out, thick_out, fields, mid, weights, ends, turned
+    gathered,
+    tracers,
+    once,
+    twice,
+    out,
+    thick_out,
+    fields,
+    cells,
+    mid,
+    weights,
+    thin,
+    ends,
+    turned,
+    staged,
+    left,
 ):
     space = lax.axis_index("space")
     tracer = lax.axis_index("tracer")
@@ -137,80 +155,164 @@
                 blocks.append(jnp.where(place >= SPAN - SIDE, above, own))
         fields[f] = jnp.concatenate(blocks, axis=0).T
 
-    row = lax.broadcasted_iota(jnp.int32, (SPAN, COLS), 0) + (space * ROWS - SIDE)
-    col = lax.broadcasted_iota(jnp.int32, (SPAN, COLS), 1)
+    def copies_out(l):
+        size = ROWS * HALVES
+        for t in range(TR):
+            at = pl.ds(pl.multiple_of((t * LEV + l) * size, size), size)
+            yield pltpu.make_async_copy(staged.at[at], out.at[at], left.at[l, t])
+
+    groups = [range(t, t + TOGETHER) for t in range(0, TR, TOGETHER)]
+    tile_shape, half_shape = (8, COLS), (SPAN, 128)
+    tile_row = lax.broadcasted_iota(jnp.int32, tile_shape, 0) + (space * ROWS - SIDE)
+    col = lax.broadcasted_iota(jnp.int32, tile_shape, 1)
+    row = lax.broadcasted_iota(jnp.int32, half_shape, 0) + (space * ROWS - SIDE)
+    near = (-3, -2, -1, 1, 2, 3)
 
     def level(l, carry):
-        at = pl.ds(pl.multiple_of(l * SPAN, SPAN), SPAN)
-        inside = (row >= 0) & (row < last_row)
-        thick = jnp.where(inside, fields[0, at, :], 1.0)
-        next_row = lambda x: pltpu.roll(x, SPAN - 1, 0)
-        next_col = lambda x: pltpu.roll(x, COLS - 1, 1)
-
-        cx = jnp.where((row > 0) & (row < last_row), COURANT_SCALE * fields[1, at, :], 0.0)
-        mfx = cx * jnp.where(cx > 0, pltpu.roll(thick, 1, 0), thick)
-        cy = jnp.where(inside & (col > 0), COURANT_SCALE * fields[2, at, :], 0.0)
-        mfy = cy * jnp.where(cy > 0, pltpu.roll(thick, 1, 1), thick)
-        thin_x = next_row(mfx) - mfx
-        thin_y = next_col(mfy) - mfy
-        dp1 = thick - thin_x
-        dp2 = dp1 - thin_y
-        dp3 = dp2 - thin_x
-        dp4 = dp3 - thin_y
-        ends[at, :] = dp4
-        r1, r2, r3, r4 = 1.0 / dp1, 1.0 / dp2, 1.0 / dp3, 1.0 / dp4
-
-        def put(n, j, add, r_a, dp_a, r_b, dp_b):
-            if j == 3:
-                weights[n, j] = (add + dp_a) * r_a
-                weights[n + 2, j] = (add + dp_b) * r_b
-            else:
-                weights[n, j] = add * r_a
-                weights[n + 2, j] = add * r_b
-
-        for j, add in enumerate(stencil(cx, mfx, next_row)):
-            put(0, j, add, r1, thick, r3, dp2)
-        for j, add in enumerate(stencil(cy, mfy, next_col)):
-            step = j - REACH
-            if step < 0:
-                add = jnp.where(col >= -step, add, 0.0)
-            elif step > 0:
-                add = jnp.where(col < COLS - step, add, 0.0)
-            put(1, j, add, r2, dp1, r4, dp3)
-
-        def weight(n, j, r):
-            return weights[n, j, r + SIDE : r + SIDE + 1, :]
-
-        def both(cells, n, r):
-            total = weight(n, 0, r) * cells[0]
-            for j in range(1, 7):
-                total += weight(n, j, r) * cells[j]
-            result = weight(n + 1, REACH, r) * total
-            for j in range(7):
-                if j != REACH:
-                    shift = (REACH - j) % COLS
-                    result += weight(n + 1, j, r) * pltpu.roll(total, shift, 1)
-            return result
-
-        def first(r):
-            if r < 0:
-                return jnp.where(odd, once[l, r + HALO], twice[l, r + HALO])
-            if r >= ROWS:
-                return jnp.where(odd, twice[l, r - ROWS], once[l, r - ROWS])
-            return get_row(tracers, l, r)
-
-        window = [first(r) for r in range(-HALO, 0)]
-        for r in range(-REACH, ROWS + REACH):
-            window.append(first(r + REACH))
-            mid[r + REACH] = both(window, 0, r)
-            window.pop(0)
-        window = [mid[r] for r in range(HALO)]
-        for r in range(ROWS):
-            window.append(mid[r + HALO])
-            done = both(window, 2, r)
-            for h in range(2):
-                out[row_of_all(l, r, h), :] = done[:, h * 128 : (h + 1) * 128]
-            window.pop(0)
+        base = pl.multiple_of(l * SPAN, SPAN)
+
+        for tile in range(SPAN // 8):
+            at = slice(8 * tile, 8 * tile + 8)
+            field = lambda f: fields[f, pl.ds(base + 8 * tile, 8), :]
+            next_col = lambda x: pltpu.roll(x, COLS - 1, 1)
+            r = tile_row + 8 * tile
+            inside = (r >= 0) & (r < last_row)
+            thick = jnp.where(inside, field(0), 1.0)
+            c = jnp.where(inside & (col > 0), COURANT_SCALE * field(2), 0.0)
+            flux = c * jnp.where(c > 0, pltpu.roll(thick, 1, 1), thick)
+            adds = stencil(c, flux, next_col)
+            values = {"thin": next_col(flux) - flux, "own": adds[REACH]}
+            for j, step in enumerate(near):
+                add = adds[step + REACH]
+                if step < 0:
+                    add = jnp.where(col >= -step, add, 0.0)
+                else:
+                    add = jnp.where(col < COLS - step, add, 0.0)
+                if abs(step) > 1:
+                    add = pltpu.roll(add, REACH if step > 0 else COLS - REACH, 1)
+                values[j] = add
+            for h in range(HALVES):
+                cut = slice(h * 128, (h + 1) * 128)
+                thin[h, at, :] = values["thin"][:, cut]
+                weights[1, 6, h, at, :] = values["own"][:, cut]
+                for j in range(6):
+                    weights[1, j, h, at, :] = values[j][:, cut]
+
+        for h in range(HALVES):
+            cut = slice(h * 128, (h + 1) * 128)
+            field = lambda f: fields[f, pl.ds(base, SPAN), cut]
+            next_row = lambda x: pltpu.roll(x, SPAN - 1, 0)
+            inside = (row >= 0) & (row < last_row)
+            thick = jnp.where(inside, field(0), 1.0)
+            c = jnp.where((row > 0) & (row < last_row), COURANT_SCALE * field(1), 0.0)
+            flux = c * jnp.where(c > 0, pltpu.roll(thick, 1, 0), thick)
+            thin_x = next_row(flux) - flux
+            adds = stencil(c, flux, next_row)
+            for j, step in enumerate(near):
+                weights[0, j, h] = adds[step + REACH]
+            thin_y = thin[h]
+            own = weights[1, 6, h]
+            for substep in range(SUBSTEPS):
+                weights[0, 6 + substep, h] = adds[REACH] + thick
+                thick = thick - thin_x
+                weights[0, 8 + substep, h] = 1.0 / thick
+                weights[1, 6 + substep, h] = own + thick
+                thick = thick - thin_y
+                weights[1, 8 + substep, h] = 1.0 / thick
+            ends[pl.ds(base, SPAN), cut] = thick
+
+        for t in range(TR):
+            for h in range(HALVES):
+                for tile in range(ROWS // 8):
+                    cells[t, h, 8 + 8 * tile : 16 + 8 * tile, :] = tracers[
+                        tile_of(t, l, tile, h), :
+                    ]
+                one, two = once[l, halo_of(t, h), :], twice[l, halo_of(t, h), :]
+                cells[t, h, 8 - HALO : 8, :] = jnp.where(odd, one, two)
+                cells[t, h, 8 + ROWS : 8 + ROWS + HALO, :] = jnp.where(odd, two, one)
+
+        def along(source, first, w):
+            total = None
+            for step in range(-REACH, REACH + 1):
+                term = w[step] * source[first + step : first + step + 8, :]
+                total = term if total is None else total + term
+            return w["over"] * total
+
+        def across(qs, w):
+            left = [pltpu.roll(q, 1, 1) for q in qs]
+            right = [pltpu.roll(q, COLS - 1, 1) for q in qs]
+            up = [w[-3] * q + w[-2] * r for q, r in zip(qs, right)]
+            down = [w[3] * q + w[2] * l for q, l in zip(qs, left)]
+            up = [pltpu.roll(x, REACH, 1) for x in up]
+            down = [pltpu.roll(x, COLS - REACH, 1) for x in down]
+            return [
+                w["over"] * (w[-1] * l + w[0] * q + w[1] * r + u + d)
+                for l, q, r, u, d in zip(left, qs, right, up, down)
+            ]
+
+        names = dict(zip(near, range(6)))
+
+        def row_weights(substep, first, h):
+            all_names = names | {0: 6 + substep, "over": 8 + substep}
+            at = slice(first, first + 8)
+            return {n: weights[0, j, h, at, :] for n, j in all_names.items()}
+
+        def col_weights(substep, first):
+            all_names = names | {0: 6 + substep, "over": 8 + substep}
+            at = slice(first, first + 8)
+            return {
+                n: jnp.concatenate([weights[1, j, h, at, :] for h in range(HALVES)], 1)
+                for n, j in all_names.items()
+            }
+
+        def mid_at(t, h, tile):
+            return mid.at[t, h, 8 * tile : 8 * tile + 8]
+
+        def staged_at(t, h, tile):
+            return staged.at[tile_of(t, l, tile, h)]
+
+        def row_steps(substep, tile):
+            first = 8 * tile + SIDE * substep
+            for h in range(HALVES):
+                w = row_weights(substep, first, h)
+                for t in range(TR):
+                    if substep == 0:
+                        source, to, start = cells.at[t, h], mid_at, first + 8 - SIDE
+                    else:
+                        source, to, start = mid.at[t, h], staged_at, first
+                    to(t, h, tile)[...] = along(source, start, w)
+                    yield
+
+        def col_steps(substep, tile):
+            w = col_weights(substep, 8 * tile + SIDE * substep)
+            at = (mid_at, staged_at)[substep]
+            for ts in groups:
+                qs = [
+                    jnp.concatenate([at(t, h, tile)[...] for h in range(HALVES)], 1)
+                    for t in ts
+                ]
+                for t, q in zip(ts, across(qs, w)):
+                    for h in range(HALVES):
+                        at(t, h, tile)[...] = q[:, h * 128 : (h + 1) * 128]
+                yield
+
+        def side_by_side(cols, rows):
+            per = TR * HALVES // len(groups)
+            while cols or rows:
+                if cols and next(cols, 0) == 0:
+                    cols = None
+                for _ in range(per):
+                    if rows and next(rows, 0) == 0:
+                        rows = None
+
+        for substep, tiles in ((0, SPAN // 8), (1, ROWS // 8)):
+            cols = None
+            for tile in range(tiles):
+                side_by_side(cols, row_steps(substep, tile))
+                cols = col_steps(substep, tile)
+            side_by_side(cols, None)
+        for copy in copies_out(l):
+            copy.start()
         return carry
 
     lax.fori_loop(0, LEV, level, 0)
@@ -219,6 +321,9 @@
     for l in range(LEV):
         start = l * SPAN + SIDE
         thick_out[l] = block[:, start : start + ROWS]
+    for l in range(LEV):
+        for copy in copies_out(l):
+            copy.wait()
 
 
 def shape(*dims):
@@ -269,7 +374,7 @@
     flat = tile_rows(tracers)
     once, twice = pl.pallas_call(
         pack_halos,
-        out_shape=[shape(LEV, HALO, TR, COLS)] * 2,
+        out_shape=[shape(LEV, TR * HALVES * HALO, 128)] * 2,
         in_specs=[VMEM],
         out_specs=[VMEM] * 2,
         compiler_params=PARAMS,
@@ -278,15 +383,19 @@
 
     values, thick = pl.pallas_call(
         sweeps,
-        out_shape=[shape(TR * LEV * ROWS * 2, 128), shape(LEV, BLOCK, ROWS)],
+        out_shape=[shape(TR * LEV * ROWS * HALVES, 128), shape(LEV, BLOCK, ROWS)],
         in_specs=[VMEM] * 4,
-        out_specs=[VMEM] * 2,
+        out_specs=[pl.BlockSpec(memory_space=pl.ANY), VMEM],
         scratch_shapes=[
             pltpu.VMEM((3, LEV * SPAN, COLS), jnp.float32),
-            pltpu.VMEM((ROWS + HALO, TR, COLS), jnp.float32),
-            pltpu.VMEM((4, 7, SPAN, COLS), jnp.float32),
+            pltpu.VMEM((TR, HALVES, ROWS + 16, 128), jnp.float32),
+            pltpu.VMEM((TR, HALVES, SPAN, 128), jnp.float32),
+            pltpu.VMEM((2, 10, HALVES, SPAN, 128), jnp.float32),
+            pltpu.VMEM((HALVES, SPAN, 128), jnp.float32),
             pltpu.VMEM((LEV * SPAN, COLS), jnp.float32),
             pltpu.VMEM((COLS, LEV * SPAN), jnp.float32),
+            pltpu.VMEM((TR * LEV * ROWS * HALVES, 128), jnp.float32),
+            pltpu.SemaphoreType.DMA((LEV, TR)),
         ],
         compiler_params=PARAMS,
     )(gathered, flat, once, twice)

time: 50.2 us -> 54.6 us (1.088)
  Pallas kernels: 7.94 us -> 12.1 us
    pallas_call x2, Pallas kernels: 5.44 us -> 9.64 us  [the longest x1 9.58 us: per_device(): pl.pallas_call(sweeps, out_shape=[shape(TR * LEV * ROWS * HALVES, 128), s...]
where the time goes in v3:
time: 54.6 us; the launch traced here: 54.2 us
  starting transfers between devices  18.4 us (34%)
  Pallas kernels  12.1 us (22%)
  waiting for transfers between devices  12.1 us (22%)
  blocking collectives  10.9 us (20%)
  between operations  0.69 us (1%)
    all_to_all x1, starting transfers between devices, per_device(): lax.all_to_all(copies, ('tracer', 'space'), 0, 0, axis_index_groups=members)  15.8 us
    all_to_all x1, waiting for transfers between devices, per_device(): lax.all_to_all(copies, ('tracer', 'space'), 0, 0, axis_index_groups=members)  12.1 us
    pallas_call x1, Pallas kernels, per_device(): pl.pallas_call(sweeps, out_shape=[shape(TR * LEV * ROWS * HALVES, 128), s...  9.58 us
    all_gather x1, blocking collectives, per_device(): pair = lax.all_gather(packed, 'tracer', axis_index_groups=same_chip)  8.58 us
    ppermute x2, starting transfers between devices, swap(): return lax.ppermute(block, 'space', pairs + [(b, a) for a, b in pairs])  2.59 us
    all_gather x1, blocking collectives, per_device(): gathered = lax.all_gather(gathered, 'tracer', axis_index_groups=same_chip)  2.36 us
    pallas_call x1, Pallas kernels, per_device(): pl.pallas_call(pack_fields, out_shape=shape(3, BLOCK, LEV * SPAN), in_spe...  1.66 us
  transfers between devices with their start and end apart: 3, of which 1 were waited for; matrix products, arithmetic and copies ran while one was open for 0% of the time, Pallas kernels for 0%

profile of v3, /device:TPU:1, one launch (start us, length us, event | category | flops | bytes accessed | tf_op | source)
XLA Modules:
  0.0 54.2 jit_solution(7310500986895462524)
XLA Ops:
  0.6 0.0 copy-start
  0.6 1.7 %shard_map.59 = f32[3,8,128]{2,1,0:T(8,128)} custom-call(f32[4,8,24]{2,1,0:T(8,128)} %bitcast.20, f32[4,8,24]{2,1,0:T(8,128)} %bitcast.21, f32[4,8,24]{2,1,0:T(8,128)} %bitcast.22), custom_call_target="tpu_custom_call" | custom-call | tf_op jit(solution)/shard_map/pallas_call | solution.py:342
  2.3 8.6 %all-gather = f32[6,8,128]{2,1,0:T(8,128)S(1)} all-gather(f32[3,8,128]{2,1,0:T(8,128)} %shard_map.59), channel_id=2, replica_groups={{0,16},{32,48},{64,80},{96,112},{128,144},{160,176},{192,208},{224,240}..., dimensions={0}, use_global_device_ids=true | all-gather | bytes 36864 | tf_op jit(solution)/shard_map/all_gather | solution.py:353
  10.9 0.8 %shard_map.60 = f32[32,24,128]{2,1,0:T(8,128)} custom-call(f32[2,3,8,128]{3,2,1,0:T(8,128)S(1)} %bitcast.19), custom_call_target="tpu_custom_call" | custom-call | tf_op jit(solution)/shard_map/pallas_call | solution.py:354
  11.7 15.8 %all-to-all-start = ((f32[32,24,128]{2,1,0:T(8,128)}), f32[32,24,128]{2,1,0:T(8,128)S(1)}, u32[]{:S(2)}, u32[]{:S(2)}) async-start(f32[32,24,128]{2,1,0:T(8,128)} %shard_map.60), calls=%async_computation | async-start | bytes 786432 | tf_op jit(solution)/shard_map/all_to_all | solution.py:369
  27.5 0.0 copy-done
  27.5 0.1 shard_map.61
  27.6 1.9 %collective-permute-start = (f32[4,96,128]{2,1,0:T(8,128)S(1)}, f32[4,96,128]{2,1,0:T(8,128)S(1)}, u32[]{:S(2)}, u32[]{:S(2)}) collective-permute-start(f32[4,96,128]{2,1,0:T(8,128)S(1)} %get-tuple-element.6), channel_id=1, source_target_pairs={{0,1},{2,3},{4,5},{6,7},{8,9},{10,11},{12,13},{14,15},{1,0},{3,2},... | collective-permute-start | bytes 589832 | tf_op jit(solution)/shard_map/ppermute | solution.py:336
  29.5 0.7 %collective-permute-start.1 = (f32[4,96,128]{2,1,0:T(8,128)S(1)}, f32[4,96,128]{2,1,0:T(8,128)S(1)}, u32[]{:S(2)}, u32[]{:S(2)}) collective-permute-start(f32[4,96,128]{2,1,0:T(8,128)S(1)} %get-tuple-element.7), channel_id=1, source_target_pairs={{1,2},{3,4},{5,6},{7,8},{9,10},{11,12},{13,14},{2,1},{4,3},{6,5},{... | collective-permute-start | bytes 589832 | tf_op jit(solution)/shard_map/ppermute | solution.py:336
  30.2 12.1 %all-to-all-done = f32[32,24,128]{2,1,0:T(8,128)S(1)} async-done(((f32[32,24,128]{2,1,0:T(8,128)}), f32[32,24,128]{2,1,0:T(8,128)S(1)}, u32[]{:S(2)}, u32[]{:S(2)}) %all-to-all-start) | async-done | bytes 393248 | tf_op jit(solution)/shard_map/all_to_all | solution.py:369
  42.3 2.4 %all-gather.1 = f32[64,24,128]{2,1,0:T(8,128)S(1)} all-gather(f32[32,24,128]{2,1,0:T(8,128)S(1)} %all-to-all-done), channel_id=3, replica_groups={{0,16},{32,48},{64,80},{96,112},{128,144},{160,176},{192,208},{224,240}..., dimensions={0}, use_global_device_ids=true | all-gather | bytes 1179648 | tf_op jit(solution)/shard_map/all_gather | solution.py:372
  44.6 0.0 collective-permute-done.once
  44.6 0.0 collective-permute-done.1.twice
  44.7 9.6 %shard_map.62 = (f32[1536,128]{1,0:T(8,128)}, f32[4,8,24]{2,1,0:T(8,128)}) custom-call(f32[2,32,24,128]{3,2,1,0:T(8,128)S(1)} %bitcast.18, f32[1536,128]{1,0:T(8,128)S(1)} %bitcast.17, f32[4,96,128]{2,1,0:T(8,128)S(1)} %collective-permute-done.once, f32[4,96,128]{2,1,0:T(8,128)S(1)} %collective-permute-done.1.twice), custom_call_target="tpu_custom_call" | custom-call | tf_op jit(solution)/shard_map/pallas_call | solution.py:384
Async XLA Ops:
  0.6 26.9 %copy-start = (f32[8,4,24,256]{3,2,1,0:T(8,128)S(1)}, f32[8,4,24,256]{3,2,1,0:T(8,128)}, u32[]{:S(2)}) copy-start(f32[8,4,24,256]{3,2,1,0:T(8,128)} %param.4) | copy-start | bytes 2359300
  11.7 30.6 %all-to-all-start = ((f32[32,24,128]{2,1,0:T(8,128)}), f32[32,24,128]{2,1,0:T(8,128)S(1)}, u32[]{:S(2)}, u32[]{:S(2)}) async-start(f32[32,24,128]{2,1,0:T(8,128)} %shard_map.60), calls=%async_computation | async-start | bytes 786432 | tf_op jit(solution)/shard_map/all_to_all | solution.py:369
  27.6 17.1 %collective-permute-start = (f32[4,96,128]{2,1,0:T(8,128)S(1)}, f32[4,96,128]{2,1,0:T(8,128)S(1)}, u32[]{:S(2)}, u32[]{:S(2)}) collective-permute-start(f32[4,96,128]{2,1,0:T(8,128)S(1)} %get-tuple-element.6), channel_id=1, source_target_pairs={{0,1},{2,3},{4,5},{6,7},{8,9},{10,11},{12,13},{14,15},{1,0},{3,2},... | collective-permute-start | bytes 589832 | tf_op jit(solution)/shard_map/ppermute | solution.py:336
  29.5 15.2 %collective-permute-start.1 = (f32[4,96,128]{2,1,0:T(8,128)S(1)}, f32[4,96,128]{2,1,0:T(8,128)S(1)}, u32[]{:S(2)}, u32[]{:S(2)}) collective-permute-start(f32[4,96,128]{2,1,0:T(8,128)S(1)} %get-tuple-element.7), channel_id=1, source_target_pairs={{1,2},{3,4},{5,6},{7,8},{9,10},{11,12},{13,14},{2,1},{4,3},{6,5},{... | collective-permute-start | bytes 589832 | tf_op jit(solution)/shard_map/ppermute | solution.py:336

commit v4 on v2

--- a/solution.py
+++ b/solution.py
@@ -7,6 +7,7 @@
 
 COURANT_SCALE = 0.025
 LEV, ROWS, COLS, TR = 4, 24, 256, 8
+FIRST = 9
 BLOCK = 8
 REACH = 3
 HALO = 2 * REACH
@@ -122,7 +123,8 @@
     for f in range(3):
         here = slice(f * BLOCK, (f + 1) * BLOCK)
         blocks = []
-        for j in range(half):
+        for chip in range(half):
+            j = (chip - FIRST) % half
             before = gathered[1, j, here, :]
             after = gathered[0, half + j, here, :]
             for own, below, above in (
@@ -253,11 +255,12 @@
         out_specs=VMEM,
         compiler_params=PARAMS,
     )(pair)
+    order = [(i + FIRST) % (count // 2) for i in range(count // 2)]
     members = [
         [
             (2 * j + core) * steps + (place + core) % steps
             for core in range(2)
-            for j in range(count // 2)
+            for j in order
         ]
         for place in range(steps)
     ]

time: 50.2 us -> 46.6 us (0.928)
  waiting for transfers between devices: 11.9 us -> 9.38 us
  starting transfers between devices: 18.4 us -> 17.3 us
    all_to_all x1, waiting for transfers between devices: 11.9 us -> 9.38 us  [per_device(): lax.all_to_all(copies, ('tracer', 'space'), 0, 0, axis_index_groups=members)]
    all_to_all x1, starting transfers between devices: 15.8 us -> 14.7 us  [per_device(): lax.all_to_all(copies, ('tracer', 'space'), 0, 0, axis_index_groups=members)]
where the time goes in v4:
time: 46.6 us; the launch traced here: 46.3 us
  starting transfers between devices  17.3 us (37%)
  blocking collectives  10.9 us (23%)
  waiting for transfers between devices  9.38 us (20%)
  Pallas kernels  7.94 us (17%)
  between operations  0.69 us (1%)
    all_to_all x1, starting transfers between devices, per_device(): lax.all_to_all(copies, ('tracer', 'space'), 0, 0, axis_index_groups=members)  14.7 us
    all_to_all x1, waiting for transfers between devices, per_device(): lax.all_to_all(copies, ('tracer', 'space'), 0, 0, axis_index_groups=members)  9.38 us
    all_gather x1, blocking collectives, per_device(): pair = lax.all_gather(packed, 'tracer', axis_index_groups=same_chip)  8.58 us
    pallas_call x1, Pallas kernels, per_device(): pl.pallas_call(sweeps, out_shape=[shape(TR * LEV * ROWS * 2, 128), shape(...  5.22 us
    ppermute x2, starting transfers between devices, swap(): return lax.ppermute(block, 'space', pairs + [(b, a) for a, b in pairs])  2.59 us
    all_gather x1, blocking collectives, per_device(): gathered = lax.all_gather(gathered, 'tracer', axis_index_groups=same_chip)  2.36 us
    pallas_call x1, Pallas kernels, per_device(): pl.pallas_call(pack_fields, out_shape=shape(3, BLOCK, LEV * SPAN), in_spe...  1.66 us
  transfers between devices with their start and end apart: 3, of which 1 were waited for; matrix products, arithmetic and copies ran while one was open for 0% of the time, Pallas kernels for 0%

profile of v4, /device:TPU:1, one launch (start us, length us, event | category | flops | bytes accessed | tf_op | source)
XLA Modules:
  0.0 46.3 jit_solution(3379418137160784548)
XLA Ops:
  0.6 0.0 copy-start
  0.6 1.7 %shard_map.59 = f32[3,8,128]{2,1,0:T(8,128)} custom-call(f32[4,8,24]{2,1,0:T(8,128)} %bitcast.20, f32[4,8,24]{2,1,0:T(8,128)} %bitcast.21, f32[4,8,24]{2,1,0:T(8,128)} %bitcast.22), custom_call_target="tpu_custom_call" | custom-call | tf_op jit(solution)/shard_map/pallas_call | solution.py:239
  2.3 8.6 %all-gather = f32[6,8,128]{2,1,0:T(8,128)S(1)} all-gather(f32[3,8,128]{2,1,0:T(8,128)} %shard_map.59), channel_id=2, replica_groups={{0,16},{32,48},{64,80},{96,112},{128,144},{160,176},{192,208},{224,240}..., dimensions={0}, use_global_device_ids=true | all-gather | bytes 36864 | tf_op jit(solution)/shard_map/all_gather | solution.py:250
  10.9 0.8 %shard_map.60 = f32[32,24,128]{2,1,0:T(8,128)} custom-call(f32[2,3,8,128]{3,2,1,0:T(8,128)S(1)} %bitcast.19), custom_call_target="tpu_custom_call" | custom-call | tf_op jit(solution)/shard_map/pallas_call | solution.py:251
  11.7 14.7 %all-to-all-start = ((f32[32,24,128]{2,1,0:T(8,128)}), f32[32,24,128]{2,1,0:T(8,128)S(1)}, u32[]{:S(2)}, u32[]{:S(2)}) async-start(f32[32,24,128]{2,1,0:T(8,128)} %shard_map.60), calls=%async_computation | async-start | bytes 786432 | tf_op jit(solution)/shard_map/all_to_all | solution.py:267
  26.5 0.0 copy-done
  26.5 0.2 shard_map.61
  26.7 1.9 %collective-permute-start = (f32[4,6,8,256]{3,2,1,0:T(8,128)S(1)}, f32[4,6,8,256]{3,2,1,0:T(8,128)S(1)}, u32[]{:S(2)}, u32[]{:S(2)}) collective-permute-start(f32[4,6,8,256]{3,2,1,0:T(8,128)S(1)} %get-tuple-element.6), channel_id=1, source_target_pairs={{0,1},{2,3},{4,5},{6,7},{8,9},{10,11},{12,13},{14,15},{1,0},{3,2},... | collective-permute-start | bytes 589832 | tf_op jit(solution)/shard_map/ppermute | solution.py:233
  28.6 0.7 %collective-permute-start.1 = (f32[4,6,8,256]{3,2,1,0:T(8,128)S(1)}, f32[4,6,8,256]{3,2,1,0:T(8,128)S(1)}, u32[]{:S(2)}, u32[]{:S(2)}) collective-permute-start(f32[4,6,8,256]{3,2,1,0:T(8,128)S(1)} %get-tuple-element.7), channel_id=1, source_target_pairs={{1,2},{3,4},{5,6},{7,8},{9,10},{11,12},{13,14},{2,1},{4,3},{6,5},{... | collective-permute-start | bytes 589832 | tf_op jit(solution)/shard_map/ppermute | solution.py:233
  29.3 9.4 %all-to-all-done = f32[32,24,128]{2,1,0:T(8,128)S(1)} async-done(((f32[32,24,128]{2,1,0:T(8,128)}), f32[32,24,128]{2,1,0:T(8,128)S(1)}, u32[]{:S(2)}, u32[]{:S(2)}) %all-to-all-start) | async-done | bytes 393248 | tf_op jit(solution)/shard_map/all_to_all | solution.py:267
  38.7 2.4 %all-gather.1 = f32[64,24,128]{2,1,0:T(8,128)S(1)} all-gather(f32[32,24,128]{2,1,0:T(8,128)S(1)} %all-to-all-done), channel_id=3, replica_groups={{0,16},{32,48},{64,80},{96,112},{128,144},{160,176},{192,208},{224,240}..., dimensions={0}, use_global_device_ids=true | all-gather | bytes 1179648 | tf_op jit(solution)/shard_map/all_gather | solution.py:270
  41.1 0.0 collective-permute-done.once
  41.1 0.0 collective-permute-done.1.twice
  41.1 5.2 %shard_map.62 = (f32[1536,128]{1,0:T(8,128)}, f32[4,8,24]{2,1,0:T(8,128)}) custom-call(f32[2,32,24,128]{3,2,1,0:T(8,128)S(1)} %bitcast.18, f32[1536,128]{1,0:T(8,128)S(1)} %bitcast.17, f32[4,6,8,256]{3,2,1,0:T(8,128)S(1)} %collective-permute-done.once, f32[4,6,8,256]{3,2,1,0:T(8,128)S(1)} %collective-permute-done.1.twice), custom_call_target="tpu_custom_call" | custom-call | tf_op jit(solution)/shard_map/pallas_call | solution.py:282
Async XLA Ops:
  0.6 25.9 %copy-start = (f32[8,4,24,256]{3,2,1,0:T(8,128)S(1)}, f32[8,4,24,256]{3,2,1,0:T(8,128)}, u32[]{:S(2)}) copy-start(f32[8,4,24,256]{3,2,1,0:T(8,128)} %param.4) | copy-start | bytes 2359300
  11.7 27.0 %all-to-all-start = ((f32[32,24,128]{2,1,0:T(8,128)}), f32[32,24,128]{2,1,0:T(8,128)S(1)}, u32[]{:S(2)}, u32[]{:S(2)}) async-start(f32[32,24,128]{2,1,0:T(8,128)} %shard_map.60), calls=%async_computation | async-start | bytes 786432 | tf_op jit(solution)/shard_map/all_to_all | solution.py:267
  26.7 14.3 %collective-permute-start = (f32[4,6,8,256]{3,2,1,0:T(8,128)S(1)}, f32[4,6,8,256]{3,2,1,0:T(8,128)S(1)}, u32[]{:S(2)}, u32[]{:S(2)}) collective-permute-start(f32[4,6,8,256]{3,2,1,0:T(8,128)S(1)} %get-tuple-element.6), channel_id=1, source_target_pairs={{0,1},{2,3},{4,5},{6,7},{8,9},{10,11},{12,13},{14,15},{1,0},{3,2},... | collective-permute-start | bytes 589832 | tf_op jit(solution)/shard_map/ppermute | solution.py:233
  28.6 12.4 %collective-permute-start.1 = (f32[4,6,8,256]{3,2,1,0:T(8,128)S(1)}, f32[4,6,8,256]{3,2,1,0:T(8,128)S(1)}, u32[]{:S(2)}, u32[]{:S(2)}) collective-permute-start(f32[4,6,8,256]{3,2,1,0:T(8,128)S(1)} %get-tuple-element.7), channel_id=1, source_target_pairs={{1,2},{3,4},{5,6},{7,8},{9,10},{11,12},{13,14},{2,1},{4,3},{6,5},{... | collective-permute-start | bytes 589832 | tf_op jit(solution)/shard_map/ppermute | solution.py:233

commit v5 on v4

--- a/solution.py
+++ b/solution.py
@@ -12,6 +12,8 @@
 REACH = 3
 HALO = 2 * REACH
 SIDE = 4
+PART = 32
+SHARE = 18
 SPAN = ROWS + 2 * SIDE
 VMEM = pl.BlockSpec(memory_space=pltpu.VMEM)
 PARAMS = pltpu.CompilerParams(vmem_limit_bytes=24 * 1024 * 1024)
@@ -24,33 +26,42 @@
     ]
     for copy in copies:
         copy.start()
-    for f, copy in enumerate(copies):
+    for copy in copies:
         copy.wait()
-        parts = []
-        for l in range(LEV):
-            own = held[f, l]
-            parts += [own[:, ROWS - SIDE :], own, own[:, :SIDE]]
-        packed[f] = jnp.concatenate(parts, axis=1)
+    whole = [jnp.concatenate([held[f, l] for l in range(LEV)], axis=1) for f in range(3)]
+    ends = [
+        [held[f, l][:, rows] for f in range(3) for l in range(LEV)]
+        for rows in (slice(ROWS - SIDE, ROWS), slice(0, SIDE))
+    ]
+    for f in range(2):
+        third = whole[2][:, f * PART : (f + 1) * PART]
+        packed[f] = jnp.concatenate([whole[f], third], axis=1)
+    packed[2] = jnp.concatenate([whole[2][:, 2 * PART :]] + ends[0] + ends[1], axis=1)
 
 
 def spread(pair, copies):
     core = lax.axis_index("tracer") % 2
-    place = lax.broadcasted_iota(jnp.int32, (BLOCK, LEV * SPAN), 1) % SPAN
-    half = copies.shape[0] // 2
-    for f in range(3):
-        here = slice(f * BLOCK, (f + 1) * BLOCK)
-        first, second = pair[0, f], pair[1, f]
-        own = jnp.where(core == 0, first, second)
-        last_rows = jnp.where(place < SIDE, first, pltpu.roll(second, SIDE, 1))
-        first_rows = jnp.where(
-            place >= SPAN - SIDE, second, pltpu.roll(first, LEV * SPAN - SIDE, 1)
-        )
-        beside = jnp.where(core == 0, last_rows, first_rows)
-        to_first = jnp.where(core == 0, own, beside)
-        to_second = jnp.where(core == 0, beside, own)
-        for i in range(half):
-            copies[i, here, :] = to_first
-            copies[half + i, here, :] = to_second
+    lane = lax.broadcasted_iota(jnp.int32, (BLOCK, 128), 1)
+    column = lax.broadcasted_iota(jnp.int32, (BLOCK, 128), 0)
+    own = [jnp.where(core == 0, pair[0, n], pair[1, n]) for n in range(3)]
+    rest = jnp.zeros((BLOCK, 128), jnp.float32)
+    for n in range(4):
+        moved = pltpu.roll(own[2], n * PART, 1) if n else own[2]
+        mine = (lane >= n * PART) & (lane < (n + 1) * PART) & (column % 4 == n)
+        rest = jnp.where(mine, moved, rest)
+    rest = [jnp.sum(rest[4 * n : 4 * n + 4], axis=0, keepdims=True) for n in range(2)]
+    first, second = pair[0, 2], pair[1, 2]
+    last_rows = jnp.where(lane < 64, pltpu.roll(first, 96, 1), pltpu.roll(second, 32, 1))
+    first_rows = jnp.where(lane < 64, pltpu.roll(second, 48, 1), pltpu.roll(first, 112, 1))
+    beside = jnp.where(core == 0, last_rows, first_rows)
+    half = copies.shape[0] // SHARE // 2
+    for i in range(2 * half):
+        at = SHARE * i
+        same = core == 0 if i < half else core == 1
+        copies[at : at + 8, :] = jnp.where(same, own[0], beside)
+        copies[at + 8 : at + 16, :] = own[1]
+        copies[at + 16 : at + 17, :] = rest[0]
+        copies[at + 17 : at + 18, :] = rest[1]
 
 
 def tile_rows(x):
@@ -118,40 +129,63 @@
     tracer = lax.axis_index("tracer")
     last_row = lax.axis_size("space") * ROWS
     odd = space % 2 == 1
-    half = gathered.shape[1] // 2
-    place = lax.broadcasted_iota(jnp.int32, (BLOCK, LEV * SPAN), 1) % SPAN
+    half = gathered.shape[1] // SHARE // 2
+    lane = lax.broadcasted_iota(jnp.int32, (BLOCK, 128), 1)
+    column = lax.broadcasted_iota(jnp.int32, (BLOCK, 128), 0)
+    blocks = [[], [], [], []]
+    for chip in range(half):
+        j = (chip - FIRST) % half
+        hers = SHARE * (half + j)
+        last_rows = gathered[1, SHARE * j : SHARE * j + 8, :]
+        first_rows = gathered[0, hers : hers + 8, :]
+        for core, at in ((0, SHARE * j), (1, hers)):
+            blocks[0].append(gathered[core, at : at + 8, :])
+            blocks[1].append(gathered[core, at + 8 : at + 16, :])
+            rest = [gathered[core, at + 16 + n : at + 17 + n, :] for n in range(2)]
+            blocks[2].append(jnp.where(column < 4, rest[0], rest[1]))
+        blocks[3].append(jnp.where(lane < 64, last_rows, first_rows))
+        blocks[3].append(jnp.where(lane < 64, first_rows, last_rows))
+    turned_to = [jnp.concatenate(b, axis=0).T for b in blocks]
+    col = lax.broadcasted_iota(jnp.int32, (PART, COLS), 1)
+    rest = turned_to[2][:PART]
+    for n in range(1, 4):
+        rest = jnp.where(col % 4 == n, turned_to[2][n * PART : (n + 1) * PART], rest)
+    whole = LEV * ROWS
+    own = [turned_to[0][:whole], turned_to[1][:whole]]
+    own.append(jnp.concatenate([turned_to[0][whole:], turned_to[1][whole:], rest], axis=0))
+    size = 3 * LEV * SIDE
+    col = lax.broadcasted_iota(jnp.int32, (size, COLS), 1)
+    on_first = (col // BLOCK) % 2 == 0
+    low_part, high_part = turned_to[3][:size], turned_to[3][64 : 64 + size]
+    below = jnp.where(on_first, low_part, high_part)
+    above = jnp.where(on_first, high_part, low_part)
     for f in range(3):
-        here = slice(f * BLOCK, (f + 1) * BLOCK)
-        blocks = []
-        for chip in range(half):
-            j = (chip - FIRST) % half
-            before = gathered[1, j, here, :]
-            after = gathered[0, half + j, here, :]
-            for own, below, above in (
-                (gathered[0, j, here, :], before, pltpu.roll(after, SIDE, 1)),
-                (
-                    gathered[1, half + j, here, :],
-                    pltpu.roll(before, LEV * SPAN - SIDE, 1),
-                    after,
-                ),
-            ):
-                own = jnp.where(place < SIDE, below, own)
-                blocks.append(jnp.where(place >= SPAN - SIDE, above, own))
-        fields[f] = jnp.concatenate(blocks, axis=0).T
+        for l in range(LEV):
+            to, side = l * SPAN, (f * LEV + l) * SIDE
+            for h in range(2):
+                cut = slice(h * 128, (h + 1) * 128)
+                fields[f, h, to : to + SIDE, :] = below[side : side + SIDE, cut]
+                fields[f, h, to + SIDE : to + SIDE + ROWS, :] = own[f][
+                    l * ROWS : (l + 1) * ROWS, cut
+                ]
+                fields[f, h, to + SIDE + ROWS : to + SPAN, :] = above[
+                    side : side + SIDE, cut
+                ]
 
     row = lax.broadcasted_iota(jnp.int32, (SPAN, COLS), 0) + (space * ROWS - SIDE)
     col = lax.broadcasted_iota(jnp.int32, (SPAN, COLS), 1)
 
     def level(l, carry):
         at = pl.ds(pl.multiple_of(l * SPAN, SPAN), SPAN)
+        field = lambda f: jnp.concatenate([fields[f, h, at, :] for h in range(2)], axis=1)
         inside = (row >= 0) & (row < last_row)
-        thick = jnp.where(inside, fields[0, at, :], 1.0)
+        thick = jnp.where(inside, field(0), 1.0)
         next_row = lambda x: pltpu.roll(x, SPAN - 1, 0)
         next_col = lambda x: pltpu.roll(x, COLS - 1, 1)
 
-        cx = jnp.where((row > 0) & (row < last_row), COURANT_SCALE * fields[1, at, :], 0.0)
+        cx = jnp.where((row > 0) & (row < last_row), COURANT_SCALE * field(1), 0.0)
         mfx = cx * jnp.where(cx > 0, pltpu.roll(thick, 1, 0), thick)
-        cy = jnp.where(inside & (col > 0), COURANT_SCALE * fields[2, at, :], 0.0)
+        cy = jnp.where(inside & (col > 0), COURANT_SCALE * field(2), 0.0)
         mfy = cy * jnp.where(cy > 0, pltpu.roll(thick, 1, 1), thick)
         thin_x = next_row(mfx) - mfx
         thin_y = next_col(mfy) - mfy
@@ -238,7 +272,7 @@
     turn = lambda x: jnp.transpose(x, (0, 2, 1))
     packed = pl.pallas_call(
         pack_fields,
-        out_shape=shape(3, BLOCK, LEV * SPAN),
+        out_shape=shape(3, BLOCK, 128),
         in_specs=[pl.BlockSpec(memory_space=pl.ANY)] * 3,
         out_specs=VMEM,
         scratch_shapes=[
@@ -250,7 +284,7 @@
     pair = lax.all_gather(packed, "tracer", axis_index_groups=same_chip)
     copies = pl.pallas_call(
         spread,
-        out_shape=shape(count, 3 * BLOCK, LEV * SPAN),
+        out_shape=shape(count * SHARE, 128),
         in_specs=[VMEM],
         out_specs=VMEM,
         compiler_params=PARAMS,
@@ -265,9 +299,14 @@
         for place in range(steps)
     ]
     gathered = lax.all_to_all(
-        copies, ("tracer", "space"), 0, 0, axis_index_groups=members
+        copies.reshape(count, 1, SHARE * 128),
+        ("tracer", "space"),
+        0,
+        0,
+        axis_index_groups=members,
     )
     gathered = lax.all_gather(gathered, "tracer", axis_index_groups=same_chip)
+    gathered = gathered.reshape(2, count * SHARE, 128)
 
     flat = tile_rows(tracers)
     once, twice = pl.pallas_call(
@@ -285,7 +324,7 @@
         in_specs=[VMEM] * 4,
         out_specs=[VMEM] * 2,
         scratch_shapes=[
-            pltpu.VMEM((3, LEV * SPAN, COLS), jnp.float32),
+            pltpu.VMEM((3, 2, LEV * SPAN, 128), jnp.float32),
             pltpu.VMEM((ROWS + HALO, TR, COLS), jnp.float32),
             pltpu.VMEM((4, 7, SPAN, COLS), jnp.float32),
             pltpu.VMEM((LEV * SPAN, COLS), jnp.float32),

time: 46.6 us -> 44.1 us (0.946)
  waiting for transfers between devices: 9.38 us -> 7.17 us
    all_to_all x1, waiting for transfers between devices: 9.38 us -> 7.17 us  [per_device(): lax.all_to_all(copies.reshape(count, 1, SHARE * 128), ('tracer', 'space')...]
  transfers between devices with their start and end apart: 3 -> 3, of which waited for: 1 -> 1; matrix products, arithmetic and copies ran while one was open for 0% -> 0% of each run, Pallas kernels for 0% -> 1%
where the time goes in v5:
time: 44.1 us; the launch traced here: 43.8 us
  starting transfers between devices  17.3 us (39%)
  blocking collectives  10.8 us (24%)
  Pallas kernels  7.78 us (18%)
  waiting for transfers between devices  7.17 us (16%)
  between operations  0.69 us (2%)
    all_to_all x1, starting transfers between devices, per_device(): lax.all_to_all(copies.reshape(count, 1, SHARE * 128), ('tracer', 'space')...  14.7 us
    all_gather x1, blocking collectives, per_device(): pair = lax.all_gather(packed, 'tracer', axis_index_groups=same_chip)  8.58 us
    all_to_all x1, waiting for transfers between devices, per_device(): lax.all_to_all(copies.reshape(count, 1, SHARE * 128), ('tracer', 'space')...  7.17 us
    pallas_call x1, Pallas kernels, per_device(): pl.pallas_call(sweeps, out_shape=[shape(TR * LEV * ROWS * 2, 128), shape(...  5.13 us
    ppermute x2, starting transfers between devices, swap(): return lax.ppermute(block, 'space', pairs + [(b, a) for a, b in pairs])  2.59 us
    all_gather x1, blocking collectives, per_device(): gathered = lax.all_gather(gathered, 'tracer', axis_index_groups=same_chip)  2.22 us
    pallas_call x1, Pallas kernels, per_device(): pl.pallas_call(pack_fields, out_shape=shape(3, BLOCK, 128), in_specs=[pl....  1.6 us
  transfers between devices with their start and end apart: 3, of which 1 were waited for; matrix products, arithmetic and copies ran while one was open for 0% of the time, Pallas kernels for 1%

profile of v5, /device:TPU:1, one launch (start us, length us, event | category | flops | bytes accessed | tf_op | source)
XLA Modules:
  0.0 43.8 jit_solution(4811861533679429872)
XLA Ops:
  0.6 0.0 copy-start
  0.6 1.6 %shard_map.59 = f32[3,8,128]{2,1,0:T(8,128)} custom-call(f32[4,8,24]{2,1,0:T(8,128)} %bitcast.21, f32[4,8,24]{2,1,0:T(8,128)} %bitcast.22, f32[4,8,24]{2,1,0:T(8,128)} %bitcast.23), custom_call_target="tpu_custom_call" | custom-call | tf_op jit(solution)/shard_map/pallas_call | solution.py:273
  2.2 8.6 %all-gather = f32[6,8,128]{2,1,0:T(8,128)S(1)} all-gather(f32[3,8,128]{2,1,0:T(8,128)} %shard_map.59), channel_id=2, replica_groups={{0,16},{32,48},{64,80},{96,112},{128,144},{160,176},{192,208},{224,240}..., dimensions={0}, use_global_device_ids=true | all-gather | bytes 36864 | tf_op jit(solution)/shard_map/all_gather | solution.py:284
  10.8 0.8 %shard_map.60 = f32[576,128]{1,0:T(8,128)} custom-call(f32[2,3,8,128]{3,2,1,0:T(8,128)S(1)} %bitcast.20), custom_call_target="tpu_custom_call" | custom-call | tf_op jit(solution)/shard_map/pallas_call | solution.py:285
  11.6 14.7 %all-to-all-start = ((f32[32,1,2304]{2,1,0:T(1,128)}), f32[32,1,2304]{2,1,0:T(1,128)S(1)}, u32[]{:S(2)}, u32[]{:S(2)}) async-start(f32[32,1,2304]{2,1,0:T(1,128)} %bitcast.4), calls=%async_computation | async-start | bytes 589824 | tf_op jit(solution)/shard_map/all_to_all | solution.py:301
  26.4 0.0 copy-done
  26.4 0.2 shard_map.61
  26.6 1.9 %collective-permute-start = (f32[4,6,8,256]{3,2,1,0:T(8,128)S(1)}, f32[4,6,8,256]{3,2,1,0:T(8,128)S(1)}, u32[]{:S(2)}, u32[]{:S(2)}) collective-permute-start(f32[4,6,8,256]{3,2,1,0:T(8,128)S(1)} %get-tuple-element.6), channel_id=1, source_target_pairs={{0,1},{2,3},{4,5},{6,7},{8,9},{10,11},{12,13},{14,15},{1,0},{3,2},... | collective-permute-start | bytes 589832 | tf_op jit(solution)/shard_map/ppermute | solution.py:267
  28.6 0.7 %collective-permute-start.1 = (f32[4,6,8,256]{3,2,1,0:T(8,128)S(1)}, f32[4,6,8,256]{3,2,1,0:T(8,128)S(1)}, u32[]{:S(2)}, u32[]{:S(2)}) collective-permute-start(f32[4,6,8,256]{3,2,1,0:T(8,128)S(1)} %get-tuple-element.7), channel_id=1, source_target_pairs={{1,2},{3,4},{5,6},{7,8},{9,10},{11,12},{13,14},{2,1},{4,3},{6,5},{... | collective-permute-start | bytes 589832 | tf_op jit(solution)/shard_map/ppermute | solution.py:267
  29.2 7.2 %all-to-all-done = f32[32,1,2304]{2,1,0:T(1,128)S(1)} async-done(((f32[32,1,2304]{2,1,0:T(1,128)}), f32[32,1,2304]{2,1,0:T(1,128)S(1)}, u32[]{:S(2)}, u32[]{:S(2)}) %all-to-all-start) | async-done | bytes 294944 | tf_op jit(solution)/shard_map/all_to_all | solution.py:301
  36.4 2.2 %all-gather.1 = f32[64,1,2304]{2,1,0:T(1,128)S(1)} all-gather(f32[32,1,2304]{2,1,0:T(1,128)S(1)} %all-to-all-done), channel_id=3, replica_groups={{0,16},{32,48},{64,80},{96,112},{128,144},{160,176},{192,208},{224,240}..., dimensions={0}, use_global_device_ids=true | all-gather | bytes 884736 | tf_op jit(solution)/shard_map/all_gather | solution.py:308
  38.6 0.0 collective-permute-done.once
  38.6 0.0 collective-permute-done.1.twice
  38.6 5.1 %shard_map.62 = (f32[1536,128]{1,0:T(8,128)}, f32[4,8,24]{2,1,0:T(8,128)}) custom-call(f32[2,576,128]{2,1,0:T(8,128)S(1)} %bitcast.19, f32[1536,128]{1,0:T(8,128)S(1)} %bitcast.18, f32[4,6,8,256]{3,2,1,0:T(8,128)S(1)} %collective-permute-done.once, f32[4,6,8,256]{3,2,1,0:T(8,128)S(1)} %collective-permute-done.1.twice), custom_call_target="tpu_custom_call" | custom-call | tf_op jit(solution)/shard_map/pallas_call | solution.py:321
Async XLA Ops:
  0.6 25.8 %copy-start = (f32[8,4,24,256]{3,2,1,0:T(8,128)S(1)}, f32[8,4,24,256]{3,2,1,0:T(8,128)}, u32[]{:S(2)}) copy-start(f32[8,4,24,256]{3,2,1,0:T(8,128)} %param.4) | copy-start | bytes 2359300
  11.6 24.8 %all-to-all-start = ((f32[32,1,2304]{2,1,0:T(1,128)}), f32[32,1,2304]{2,1,0:T(1,128)S(1)}, u32[]{:S(2)}, u32[]{:S(2)}) async-start(f32[32,1,2304]{2,1,0:T(1,128)} %bitcast.4), calls=%async_computation | async-start | bytes 589824 | tf_op jit(solution)/shard_map/all_to_all | solution.py:301
  26.6 12.0 %collective-permute-start = (f32[4,6,8,256]{3,2,1,0:T(8,128)S(1)}, f32[4,6,8,256]{3,2,1,0:T(8,128)S(1)}, u32[]{:S(2)}, u32[]{:S(2)}) collective-permute-start(f32[4,6,8,256]{3,2,1,0:T(8,128)S(1)} %get-tuple-element.6), channel_id=1, source_target_pairs={{0,1},{2,3},{4,5},{6,7},{8,9},{10,11},{12,13},{14,15},{1,0},{3,2},... | collective-permute-start | bytes 589832 | tf_op jit(solution)/shard_map/ppermute | solution.py:267
  28.6 10.1 %collective-permute-start.1 = (f32[4,6,8,256]{3,2,1,0:T(8,128)S(1)}, f32[4,6,8,256]{3,2,1,0:T(8,128)S(1)}, u32[]{:S(2)}, u32[]{:S(2)}) collective-permute-start(f32[4,6,8,256]{3,2,1,0:T(8,128)S(1)} %get-tuple-element.7), channel_id=1, source_target_pairs={{1,2},{3,4},{5,6},{7,8},{9,10},{11,12},{13,14},{2,1},{4,3},{6,5},{... | collective-permute-start | bytes 589832 | tf_op jit(solution)/shard_map/ppermute | solution.py:267

commit v6 on v5

--- a/solution.py
+++ b/solution.py
@@ -6,8 +6,10 @@
 from jax.sharding import PartitionSpec as P
 
 COURANT_SCALE = 0.025
+SUBSTEPS = 2
 LEV, ROWS, COLS, TR = 4, 24, 256, 8
-FIRST = 9
+LEAD = 1
+FIRST = 11
 BLOCK = 8
 REACH = 3
 HALO = 2 * REACH
@@ -19,45 +21,40 @@
 PARAMS = pltpu.CompilerParams(vmem_limit_bytes=24 * 1024 * 1024)
 
 
-def pack_fields(thick, wind_x, wind_y, packed, held, arrived):
-    copies = [
-        pltpu.make_async_copy(field, held.at[f], arrived.at[f])
-        for f, field in enumerate((thick, wind_x, wind_y))
-    ]
-    for copy in copies:
-        copy.start()
-    for copy in copies:
-        copy.wait()
-    whole = [jnp.concatenate([held[f, l] for l in range(LEV)], axis=1) for f in range(3)]
+def packed(fields):
+    whole = [jnp.concatenate([fields[f, l] for l in range(LEV)], axis=1) for f in range(3)]
     ends = [
-        [held[f, l][:, rows] for f in range(3) for l in range(LEV)]
+        [fields[f, l][:, rows] for f in range(3) for l in range(LEV)]
         for rows in (slice(ROWS - SIDE, ROWS), slice(0, SIDE))
     ]
-    for f in range(2):
-        third = whole[2][:, f * PART : (f + 1) * PART]
-        packed[f] = jnp.concatenate([whole[f], third], axis=1)
-    packed[2] = jnp.concatenate([whole[2][:, 2 * PART :]] + ends[0] + ends[1], axis=1)
+    thirds = [whole[2][:, n * PART : (n + 1) * PART] for n in range(3)]
+    return [
+        jnp.concatenate([whole[0], thirds[0]], axis=1),
+        jnp.concatenate([whole[1], thirds[1]], axis=1),
+        jnp.concatenate([thirds[2]] + ends[0] + ends[1], axis=1),
+    ]
 
 
 def spread(pair, copies):
     core = lax.axis_index("tracer") % 2
     lane = lax.broadcasted_iota(jnp.int32, (BLOCK, 128), 1)
     column = lax.broadcasted_iota(jnp.int32, (BLOCK, 128), 0)
-    own = [jnp.where(core == 0, pair[0, n], pair[1, n]) for n in range(3)]
+    both = [packed(pair.at[n]) for n in range(2)]
+    own = [jnp.where(core == 0, a, b) for a, b in zip(*both)]
     rest = jnp.zeros((BLOCK, 128), jnp.float32)
     for n in range(4):
         moved = pltpu.roll(own[2], n * PART, 1) if n else own[2]
         mine = (lane >= n * PART) & (lane < (n + 1) * PART) & (column % 4 == n)
         rest = jnp.where(mine, moved, rest)
     rest = [jnp.sum(rest[4 * n : 4 * n + 4], axis=0, keepdims=True) for n in range(2)]
-    first, second = pair[0, 2], pair[1, 2]
+    first, second = both[0][2], both[1][2]
     last_rows = jnp.where(lane < 64, pltpu.roll(first, 96, 1), pltpu.roll(second, 32, 1))
     first_rows = jnp.where(lane < 64, pltpu.roll(second, 48, 1), pltpu.roll(first, 112, 1))
     beside = jnp.where(core == 0, last_rows, first_rows)
     half = copies.shape[0] // SHARE // 2
     for i in range(2 * half):
         at = SHARE * i
-        same = core == 0 if i < half else core == 1
+        same = core == (LEAD if i < half else 1 - LEAD)
         copies[at : at + 8, :] = jnp.where(same, own[0], beside)
         copies[at + 8 : at + 16, :] = own[1]
         copies[at + 16 : at + 17, :] = rest[0]
@@ -95,31 +92,28 @@
 
 def stencil(courant, flux, after):
     size = jnp.abs(courant)
-    half = 0.5 * size
-    curve = 3.0 * half * (1.0 - (2.0 / 3.0) * size)
-    near = flux * (1.0 - half - curve)
-    far = flux * (half - curve)
-    mean = flux * (2.0 * curve)
+    rest = 1.0 - size
+    part = flux * rest * (1.0 / 12.0)
+    near, far = part * rest, part * size
+    mean = flux - 12.0 * (near - far)
     up = courant > 0
     far_l = jnp.where(up, far, 0.0)
     far_r = far - far_l
     mean_l = jnp.where(up, mean, 0.0)
     mean_r = mean - mean_l
-    in_, out = 7.0 / 12.0, 1.0 / 12.0
-    face = [
-        -out * far_l,
-        in_ * far_l - out * near,
-        in_ * (far_l + near) - out * far_r + mean_l,
-        in_ * (far_r + near) - out * far_l + mean_r,
-        in_ * far_r - out * near,
-        -out * far_r,
+    near7, left7, right7 = 7.0 * near, 7.0 * far_l, 7.0 * far_r
+    outer_l, outer_r = left7 + near, right7 + near
+    inner_l = (near7 - left7) + (far_r + mean_l)
+    inner_r = (near7 - right7) + (far_l + mean_r)
+    return [
+        (far_l, 1),
+        (outer_l + after(far_l), -1),
+        (inner_l + after(outer_l), 1),
+        (inner_r - after(inner_l), 1),
+        (outer_r + after(inner_r), -1),
+        (far_r + after(outer_r), 1),
+        (after(far_r), -1),
     ]
-    moved = [after(w) for w in face]
-    return (
-        [face[0]]
-        + [face[j] - moved[j - 1] for j in range(1, 6)]
-        + [-moved[5]]
-    )
 
 
 def sweeps(
@@ -135,10 +129,10 @@
     blocks = [[], [], [], []]
     for chip in range(half):
         j = (chip - FIRST) % half
-        hers = SHARE * (half + j)
-        last_rows = gathered[1, SHARE * j : SHARE * j + 8, :]
-        first_rows = gathered[0, hers : hers + 8, :]
-        for core, at in ((0, SHARE * j), (1, hers)):
+        places = [SHARE * (j + (0 if core == LEAD else half)) for core in range(2)]
+        last_rows = gathered[1, places[0] : places[0] + 8, :]
+        first_rows = gathered[0, places[1] : places[1] + 8, :]
+        for core, at in enumerate(places):
             blocks[0].append(gathered[core, at : at + 8, :])
             blocks[1].append(gathered[core, at + 8 : at + 16, :])
             rest = [gathered[core, at + 16 + n : at + 17 + n, :] for n in range(2)]
@@ -194,39 +188,51 @@
         dp3 = dp2 - thin_x
         dp4 = dp3 - thin_y
         ends[at, :] = dp4
-        r1, r2, r3, r4 = 1.0 / dp1, 1.0 / dp2, 1.0 / dp3, 1.0 / dp4
-
-        def put(n, j, add, r_a, dp_a, r_b, dp_b):
-            if j == 3:
-                weights[n, j] = (add + dp_a) * r_a
-                weights[n + 2, j] = (add + dp_b) * r_b
-            else:
-                weights[n, j] = add * r_a
-                weights[n + 2, j] = add * r_b
-
-        for j, add in enumerate(stencil(cx, mfx, next_row)):
-            put(0, j, add, r1, thick, r3, dp2)
-        for j, add in enumerate(stencil(cy, mfy, next_col)):
-            step = j - REACH
-            if step < 0:
-                add = jnp.where(col >= -step, add, 0.0)
-            elif step > 0:
-                add = jnp.where(col < COLS - step, add, 0.0)
-            put(1, j, add, r2, dp1, r4, dp3)
+        def put(n, adds, starts, results, placed):
+            for substep in range(SUBSTEPS):
+                over = 1.0 / results[substep]
+                signed = {1: over, -1: -over}
+                for j, (add, sign) in enumerate(adds):
+                    if j == REACH:
+                        add = add + starts[substep]
+                    weights[2 * substep + n, j] = placed(j - REACH, add * signed[sign])
+
+        def inside_only(adds):
+            for j, (add, sign) in enumerate(adds):
+                step = j - REACH
+                if step < 0:
+                    add = jnp.where(col >= -step, add, 0.0)
+                elif step > 0:
+                    add = jnp.where(col < COLS - step, add, 0.0)
+                yield add, sign
+
+        def placed(step, value):
+            if abs(step) > 1:
+                value = pltpu.roll(value, REACH if step > 0 else COLS - REACH, 1)
+            return value
+
+        put(0, stencil(cx, mfx, next_row), (thick, dp2), (dp1, dp3), lambda _, x: x)
+        y_adds = list(inside_only(stencil(cy, mfy, next_col)))
+        put(1, y_adds, (dp1, dp3), (dp2, dp4), placed)
 
         def weight(n, j, r):
             return weights[n, j, r + SIDE : r + SIDE + 1, :]
 
-        def both(cells, n, r):
-            total = weight(n, 0, r) * cells[0]
-            for j in range(1, 7):
-                total += weight(n, j, r) * cells[j]
-            result = weight(n + 1, REACH, r) * total
-            for j in range(7):
-                if j != REACH:
-                    shift = (REACH - j) % COLS
-                    result += weight(n + 1, j, r) * pltpu.roll(total, shift, 1)
-            return result
+        def along(cells, substep, r):
+            total = weight(2 * substep, 0, r) * cells[0]
+            for j in range(1, 2 * REACH + 1):
+                total += weight(2 * substep, j, r) * cells[j]
+            return total
+
+        def begin(q, substep, r):
+            w = lambda j: weight(2 * substep + 1, j, r)
+            left, right = pltpu.roll(q, 1, 1), next_col(q)
+            up = w(0) * q + w(1) * right
+            down = w(6) * q + w(5) * left
+            return w(3) * q + w(2) * left + w(4) * right, up, down
+
+        def end(total, up, down):
+            return total + (pltpu.roll(up, REACH, 1) + pltpu.roll(down, COLS - REACH, 1))
 
         def first(r):
             if r < 0:
@@ -235,18 +241,54 @@
                 return jnp.where(odd, twice[l, r - ROWS], once[l, r - ROWS])
             return get_row(tracers, l, r)
 
-        window = [first(r) for r in range(-HALO, 0)]
-        for r in range(-REACH, ROWS + REACH):
-            window.append(first(r + REACH))
-            mid[r + REACH] = both(window, 0, r)
-            window.pop(0)
-        window = [mid[r] for r in range(HALO)]
-        for r in range(ROWS):
-            window.append(mid[r + HALO])
-            done = both(window, 2, r)
+        def staged(rows, start, stages):
+            rows = list(rows)
+            held = [dict() for _ in stages]
+            for n in range(len(rows) + 14 * (len(stages) - 1)):
+                for k, stage in enumerate(stages):
+                    at = n - 14 * k
+                    if 0 <= at < len(rows):
+                        args = held[k - 1].pop(at) if k else start(rows[at])
+                        held[k][at] = stage(rows[at], *args)
+
+        def keep_mid(r, *parts):
+            mid[r + REACH] = end(*parts)
+
+        def keep_out(r, *parts):
+            done = end(*parts)
             for h in range(2):
                 out[row_of_all(l, r, h), :] = done[:, h * 128 : (h + 1) * 128]
-            window.pop(0)
+
+        window = [first(r) for r in range(-HALO, 0)]
+
+        def next_first(r):
+            window.append(first(r + REACH))
+            return (list(window[-7:]),)
+
+        staged(
+            range(-REACH, ROWS + REACH),
+            next_first,
+            [
+                lambda r, cells: (along(cells, 0, r),),
+                lambda r, q: begin(q, 0, r),
+                keep_mid,
+            ],
+        )
+        window = [mid[r] for r in range(HALO)]
+
+        def next_mid(r):
+            window.append(mid[r + HALO])
+            return (list(window[-7:]),)
+
+        staged(
+            range(ROWS),
+            next_mid,
+            [
+                lambda r, cells: (along(cells, 1, r),),
+                lambda r, q: begin(q, 1, r),
+                keep_out,
+            ],
+        )
         return carry
 
     lax.fori_loop(0, LEV, level, 0)
@@ -270,18 +312,9 @@
 def per_device(tracers, thickness, wind_x, wind_y):
     count, steps = lax.axis_size("tracer"), lax.axis_size("space")
     turn = lambda x: jnp.transpose(x, (0, 2, 1))
-    packed = pl.pallas_call(
-        pack_fields,
-        out_shape=shape(3, BLOCK, 128),
-        in_specs=[pl.BlockSpec(memory_space=pl.ANY)] * 3,
-        out_specs=VMEM,
-        scratch_shapes=[
-            pltpu.VMEM((3, LEV, BLOCK, ROWS), jnp.float32),
-            pltpu.SemaphoreType.DMA((3,)),
-        ],
-    )(turn(thickness), turn(wind_x), turn(wind_y))
+    fields = jnp.stack([turn(thickness), turn(wind_x), turn(wind_y)])
     same_chip = [[i, i + 1] for i in range(0, count, 2)]
-    pair = lax.all_gather(packed, "tracer", axis_index_groups=same_chip)
+    pair = lax.all_gather(fields, "tracer", axis_index_groups=same_chip)
     copies = pl.pallas_call(
         spread,
         out_shape=shape(count * SHARE, 128),
@@ -293,7 +326,7 @@
     members = [
         [
             (2 * j + core) * steps + (place + core) % steps
-            for core in range(2)
+            for core in (LEAD, 1 - LEAD)
             for j in order
         ]
         for place in range(steps)

time: 44.1 us -> 42.2 us (0.957)
  Pallas kernels: 7.78 us -> 5.82 us
  waiting for transfers between devices: 7.17 us -> 5.86 us
  other arithmetic: 0 us -> 0.83 us
  starting transfers between devices: 17.3 us -> 18.1 us
    pallas_call x1 -> x0, Pallas kernels: 1.6 us -> none  [per_device(): pl.pallas_call(pack_fields, out_shape=shape(3, BLOCK, 128), in_specs=[pl....]
    all_to_all x1, waiting for transfers between devices: 7.17 us -> 5.86 us  [per_device(): lax.all_to_all(copies.reshape(count, 1, SHARE * 128), ('tracer', 'space')...]
    another operation x0 -> x1, other arithmetic: none -> 0.83 us  [per_device(): fields = jnp.stack([turn(thickness), turn(wind_x), turn(wind_y)])]
    all_to_all x1, starting transfers between devices: 14.7 us -> 15.5 us  [per_device(): lax.all_to_all(copies.reshape(count, 1, SHARE * 128), ('tracer', 'space')...]
    pallas_call x1, Pallas kernels: 5.13 us -> 4.62 us  [per_device(): pl.pallas_call(sweeps, out_shape=[shape(TR * LEV * ROWS * 2, 128), shape(...]
where the time goes in v6:
time: 42.2 us; the launch traced here: 41.9 us
  starting transfers between devices  18.1 us (43%)
  blocking collectives  10.6 us (25%)
  waiting for transfers between devices  5.86 us (14%)
  Pallas kernels  5.82 us (14%)
  other arithmetic  0.83 us (2%)
  between operations  0.68 us (2%)
    all_to_all x1, starting transfers between devices, per_device(): lax.all_to_all(copies.reshape(count, 1, SHARE * 128), ('tracer', 'space')...  15.5 us
    all_gather x1, blocking collectives, per_device(): pair = lax.all_gather(fields, 'tracer', axis_index_groups=same_chip)  8.39 us
    all_to_all x1, waiting for transfers between devices, per_device(): lax.all_to_all(copies.reshape(count, 1, SHARE * 128), ('tracer', 'space')...  5.86 us
    pallas_call x1, Pallas kernels, per_device(): pl.pallas_call(sweeps, out_shape=[shape(TR * LEV * ROWS * 2, 128), shape(...  4.62 us
    ppermute x2, starting transfers between devices, swap(): return lax.ppermute(block, 'space', pairs + [(b, a) for a, b in pairs])  2.59 us
    all_gather x1, blocking collectives, per_device(): gathered = lax.all_gather(gathered, 'tracer', axis_index_groups=same_chip)  2.22 us
    pallas_call x1, Pallas kernels, per_device(): pl.pallas_call(spread, out_shape=shape(count * SHARE, 128), in_specs=[VME...  0.98 us
  transfers between devices with their start and end apart: 3, of which 1 were waited for; matrix products, arithmetic and copies ran while one was open for 0% of the time, Pallas kernels for 1%

profile of v6, /device:TPU:1, one launch (start us, length us, event | category | flops | bytes accessed | tf_op | source)
XLA Modules:
  0.0 41.9 jit_solution(1876772207977541247)
XLA Ops:
  0.6 0.0 copy-start
  0.6 0.8 %pad_maximum_fusion = f32[3,4,8,24]{3,2,1,0:T(8,128)S(1)} fusion(f32[1,4,8,24]{3,2,1,0:T(8,128)} %bitcast.27, f32[1,4,8,24]{3,2,1,0:T(8,128)} %bitcast.28, f32[1,4,8,24]{3,2,1,0:T(8,128)} %bitcast.29), kind=kLoop, calls=%fused_computation | loop fusion | flops 4608 | bytes 18432 | tf_op jit(solution)/shard_map/stack | solution.py:315
  1.5 8.4 %all-gather = f32[6,4,8,24]{3,2,1,0:T(8,128)S(1)} all-gather(f32[3,4,8,24]{3,2,1,0:T(8,128)S(1)} %pad_maximum_fusion), channel_id=2, replica_groups={{0,16},{32,48},{64,80},{96,112},{128,144},{160,176},{192,208},{224,240}..., dimensions={0}, use_global_device_ids=true | all-gather | bytes 27648 | tf_op jit(solution)/shard_map/all_gather | solution.py:317
  9.9 1.0 %shard_map.59 = f32[576,128]{1,0:T(8,128)} custom-call(f32[2,3,4,8,24]{4,3,2,1,0:T(8,128)S(1)} %bitcast.26), custom_call_target="tpu_custom_call" | custom-call | tf_op jit(solution)/shard_map/pallas_call | solution.py:318
  10.8 15.5 %all-to-all-start = ((f32[32,1,2304]{2,1,0:T(1,128)}), f32[32,1,2304]{2,1,0:T(1,128)S(1)}, u32[]{:S(2)}, u32[]{:S(2)}) async-start(f32[32,1,2304]{2,1,0:T(1,128)} %bitcast.7), calls=%async_computation | async-start | bytes 589824 | tf_op jit(solution)/shard_map/all_to_all | solution.py:334
  26.3 0.0 copy-done
  26.3 0.2 shard_map.60
  26.6 1.9 %collective-permute-start = (f32[4,6,8,256]{3,2,1,0:T(8,128)S(1)}, f32[4,6,8,256]{3,2,1,0:T(8,128)S(1)}, u32[]{:S(2)}, u32[]{:S(2)}) collective-permute-start(f32[4,6,8,256]{3,2,1,0:T(8,128)S(1)} %get-tuple-element.6), channel_id=1, source_target_pairs={{0,1},{2,3},{4,5},{6,7},{8,9},{10,11},{12,13},{14,15},{1,0},{3,2},... | collective-permute-start | bytes 589832 | tf_op jit(solution)/shard_map/ppermute | solution.py:309
  28.5 0.7 %collective-permute-start.1 = (f32[4,6,8,256]{3,2,1,0:T(8,128)S(1)}, f32[4,6,8,256]{3,2,1,0:T(8,128)S(1)}, u32[]{:S(2)}, u32[]{:S(2)}) collective-permute-start(f32[4,6,8,256]{3,2,1,0:T(8,128)S(1)} %get-tuple-element.7), channel_id=1, source_target_pairs={{1,2},{3,4},{5,6},{7,8},{9,10},{11,12},{13,14},{2,1},{4,3},{6,5},{... | collective-permute-start | bytes 589832 | tf_op jit(solution)/shard_map/ppermute | solution.py:309
  29.2 5.9 %all-to-all-done = f32[32,1,2304]{2,1,0:T(1,128)S(1)} async-done(((f32[32,1,2304]{2,1,0:T(1,128)}), f32[32,1,2304]{2,1,0:T(1,128)S(1)}, u32[]{:S(2)}, u32[]{:S(2)}) %all-to-all-start) | async-done | bytes 294944 | tf_op jit(solution)/shard_map/all_to_all | solution.py:334
  35.0 2.2 %all-gather.1 = f32[64,1,2304]{2,1,0:T(1,128)S(1)} all-gather(f32[32,1,2304]{2,1,0:T(1,128)S(1)} %all-to-all-done), channel_id=3, replica_groups={{0,16},{32,48},{64,80},{96,112},{128,144},{160,176},{192,208},{224,240}..., dimensions={0}, use_global_device_ids=true | all-gather | bytes 884736 | tf_op jit(solution)/shard_map/all_gather | solution.py:341
  37.3 0.0 collective-permute-done.once
  37.3 0.0 collective-permute-done.1.twice
  37.3 4.6 %shard_map.61 = (f32[1536,128]{1,0:T(8,128)}, f32[4,8,24]{2,1,0:T(8,128)}) custom-call(f32[2,576,128]{2,1,0:T(8,128)S(1)} %bitcast.25, f32[1536,128]{1,0:T(8,128)S(1)} %bitcast.24, f32[4,6,8,256]{3,2,1,0:T(8,128)S(1)} %collective-permute-done.once, f32[4,6,8,256]{3,2,1,0:T(8,128)S(1)} %collective-permute-done.1.twice), custom_call_target="tpu_custom_call" | custom-call | tf_op jit(solution)/shard_map/pallas_call | solution.py:354
Async XLA Ops:
  0.6 25.7 %copy-start = (f32[8,4,24,256]{3,2,1,0:T(8,128)S(1)}, f32[8,4,24,256]{3,2,1,0:T(8,128)}, u32[]{:S(2)}) copy-start(f32[8,4,24,256]{3,2,1,0:T(8,128)} %param.4) | copy-start | bytes 2359300
  10.8 24.2 %all-to-all-start = ((f32[32,1,2304]{2,1,0:T(1,128)}), f32[32,1,2304]{2,1,0:T(1,128)S(1)}, u32[]{:S(2)}, u32[]{:S(2)}) async-start(f32[32,1,2304]{2,1,0:T(1,128)} %bitcast.7), calls=%async_computation | async-start | bytes 589824 | tf_op jit(solution)/shard_map/all_to_all | solution.py:334
  26.6 10.7 %collective-permute-start = (f32[4,6,8,256]{3,2,1,0:T(8,128)S(1)}, f32[4,6,8,256]{3,2,1,0:T(8,128)S(1)}, u32[]{:S(2)}, u32[]{:S(2)}) collective-permute-start(f32[4,6,8,256]{3,2,1,0:T(8,128)S(1)} %get-tuple-element.6), channel_id=1, source_target_pairs={{0,1},{2,3},{4,5},{6,7},{8,9},{10,11},{12,13},{14,15},{1,0},{3,2},... | collective-permute-start | bytes 589832 | tf_op jit(solution)/shard_map/ppermute | solution.py:309
  28.5 8.8 %collective-permute-start.1 = (f32[4,6,8,256]{3,2,1,0:T(8,128)S(1)}, f32[4,6,8,256]{3,2,1,0:T(8,128)S(1)}, u32[]{:S(2)}, u32[]{:S(2)}) collective-permute-start(f32[4,6,8,256]{3,2,1,0:T(8,128)S(1)} %get-tuple-element.7), channel_id=1, source_target_pairs={{1,2},{3,4},{5,6},{7,8},{9,10},{11,12},{13,14},{2,1},{4,3},{6,5},{... | collective-permute-start | bytes 589832 | tf_op jit(solution)/shard_map/ppermute | solution.py:309

commit v7 on v6

--- a/solution.py
+++ b/solution.py
@@ -19,6 +19,10 @@
 SPAN = ROWS + 2 * SIDE
 VMEM = pl.BlockSpec(memory_space=pltpu.VMEM)
 PARAMS = pltpu.CompilerParams(vmem_limit_bytes=24 * 1024 * 1024)
+
+
+def listed(chips):
+    return [(i + FIRST) % chips for i in range(chips)]
 
 
 def packed(fields):
@@ -54,7 +58,7 @@
     half = copies.shape[0] // SHARE // 2
     for i in range(2 * half):
         at = SHARE * i
-        same = core == (LEAD if i < half else 1 - LEAD)
+        same = core == (LEAD if i % 2 == 0 else 1 - LEAD)
         copies[at : at + 8, :] = jnp.where(same, own[0], beside)
         copies[at + 8 : at + 16, :] = own[1]
         copies[at + 16 : at + 17, :] = rest[0]
@@ -128,8 +132,8 @@
     column = lax.broadcasted_iota(jnp.int32, (BLOCK, 128), 0)
     blocks = [[], [], [], []]
     for chip in range(half):
-        j = (chip - FIRST) % half
-        places = [SHARE * (j + (0 if core == LEAD else half)) for core in range(2)]
+        j = listed(half).index(chip)
+        places = [SHARE * (2 * j + (0 if core == LEAD else 1)) for core in range(2)]
         last_rows = gathered[1, places[0] : places[0] + 8, :]
         first_rows = gathered[0, places[1] : places[1] + 8, :]
         for core, at in enumerate(places):
@@ -322,12 +326,12 @@
         out_specs=VMEM,
         compiler_params=PARAMS,
     )(pair)
-    order = [(i + FIRST) % (count // 2) for i in range(count // 2)]
+    order = listed(count // 2)
     members = [
         [
             (2 * j + core) * steps + (place + core) % steps
+            for j in order
             for core in (LEAD, 1 - LEAD)
-            for j in order
         ]
         for place in range(steps)
     ]

time: 42.2 us -> 42.2 us (level)
  no operation moved by 1% of the time
where the time goes in v7:
time: 42.2 us; the launch traced here: 41.9 us
  starting transfers between devices  18.1 us (43%)
  blocking collectives  10.6 us (25%)
  waiting for transfers between devices  5.84 us (14%)
  Pallas kernels  5.82 us (14%)
  other arithmetic  0.83 us (2%)
  between operations  0.68 us (2%)
    all_to_all x1, starting transfers between devices, per_device(): lax.all_to_all(copies.reshape(count, 1, SHARE * 128), ('tracer', 'space')...  15.5 us
    all_gather x1, blocking collectives, per_device(): pair = lax.all_gather(fields, 'tracer', axis_index_groups=same_chip)  8.39 us
    all_to_all x1, waiting for transfers between devices, per_device(): lax.all_to_all(copies.reshape(count, 1, SHARE * 128), ('tracer', 'space')...  5.83 us
    pallas_call x1, Pallas kernels, per_device(): pl.pallas_call(sweeps, out_shape=[shape(TR * LEV * ROWS * 2, 128), shape(...  4.62 us
    ppermute x2, starting transfers between devices, swap(): return lax.ppermute(block, 'space', pairs + [(b, a) for a, b in pairs])  2.59 us
    all_gather x1, blocking collectives, per_device(): gathered = lax.all_gather(gathered, 'tracer', axis_index_groups=same_chip)  2.22 us
    pallas_call x1, Pallas kernels, per_device(): pl.pallas_call(spread, out_shape=shape(count * SHARE, 128), in_specs=[VME...  0.98 us
  transfers between devices with their start and end apart: 3, of which 1 were waited for; matrix products, arithmetic and copies ran while one was open for 0% of the time, Pallas kernels for 1%

profile of v7, /device:TPU:1, one launch (start us, length us, event | category | flops | bytes accessed | tf_op | source)
XLA Modules:
  0.0 41.9 jit_solution(10349958721830608413)
XLA Ops:
  0.6 0.0 copy-start
  0.6 0.8 %pad_maximum_fusion = f32[3,4,8,24]{3,2,1,0:T(8,128)S(1)} fusion(f32[1,4,8,24]{3,2,1,0:T(8,128)} %bitcast.27, f32[1,4,8,24]{3,2,1,0:T(8,128)} %bitcast.28, f32[1,4,8,24]{3,2,1,0:T(8,128)} %bitcast.29), kind=kLoop, calls=%fused_computation | loop fusion | flops 4608 | bytes 18432 | tf_op jit(solution)/shard_map/stack | solution.py:319
  1.5 8.4 %all-gather = f32[6,4,8,24]{3,2,1,0:T(8,128)S(1)} all-gather(f32[3,4,8,24]{3,2,1,0:T(8,128)S(1)} %pad_maximum_fusion), channel_id=2, replica_groups={{0,16},{32,48},{64,80},{96,112},{128,144},{160,176},{192,208},{224,240}..., dimensions={0}, use_global_device_ids=true | all-gather | bytes 27648 | tf_op jit(solution)/shard_map/all_gather | solution.py:321
  9.9 1.0 %shard_map.59 = f32[576,128]{1,0:T(8,128)} custom-call(f32[2,3,4,8,24]{4,3,2,1,0:T(8,128)S(1)} %bitcast.26), custom_call_target="tpu_custom_call" | custom-call | tf_op jit(solution)/shard_map/pallas_call | solution.py:322
  10.8 15.5 %all-to-all-start = ((f32[32,1,2304]{2,1,0:T(1,128)}), f32[32,1,2304]{2,1,0:T(1,128)S(1)}, u32[]{:S(2)}, u32[]{:S(2)}) async-start(f32[32,1,2304]{2,1,0:T(1,128)} %bitcast.7), calls=%async_computation | async-start | bytes 589824 | tf_op jit(solution)/shard_map/all_to_all | solution.py:338
  26.3 0.0 copy-done
  26.4 0.2 shard_map.60
  26.6 1.9 %collective-permute-start = (f32[4,6,8,256]{3,2,1,0:T(8,128)S(1)}, f32[4,6,8,256]{3,2,1,0:T(8,128)S(1)}, u32[]{:S(2)}, u32[]{:S(2)}) collective-permute-start(f32[4,6,8,256]{3,2,1,0:T(8,128)S(1)} %get-tuple-element.6), channel_id=1, source_target_pairs={{0,1},{2,3},{4,5},{6,7},{8,9},{10,11},{12,13},{14,15},{1,0},{3,2},... | collective-permute-start | bytes 589832 | tf_op jit(solution)/shard_map/ppermute | solution.py:313
  28.5 0.7 %collective-permute-start.1 = (f32[4,6,8,256]{3,2,1,0:T(8,128)S(1)}, f32[4,6,8,256]{3,2,1,0:T(8,128)S(1)}, u32[]{:S(2)}, u32[]{:S(2)}) collective-permute-start(f32[4,6,8,256]{3,2,1,0:T(8,128)S(1)} %get-tuple-element.7), channel_id=1, source_target_pairs={{1,2},{3,4},{5,6},{7,8},{9,10},{11,12},{13,14},{2,1},{4,3},{6,5},{... | collective-permute-start | bytes 589832 | tf_op jit(solution)/shard_map/ppermute | solution.py:313
  29.2 5.8 %all-to-all-done = f32[32,1,2304]{2,1,0:T(1,128)S(1)} async-done(((f32[32,1,2304]{2,1,0:T(1,128)}), f32[32,1,2304]{2,1,0:T(1,128)S(1)}, u32[]{:S(2)}, u32[]{:S(2)}) %all-to-all-start) | async-done | bytes 294944 | tf_op jit(solution)/shard_map/all_to_all | solution.py:338
  35.0 2.2 %all-gather.1 = f32[64,1,2304]{2,1,0:T(1,128)S(1)} all-gather(f32[32,1,2304]{2,1,0:T(1,128)S(1)} %all-to-all-done), channel_id=3, replica_groups={{0,16},{32,48},{64,80},{96,112},{128,144},{160,176},{192,208},{224,240}..., dimensions={0}, use_global_device_ids=true | all-gather | bytes 884736 | tf_op jit(solution)/shard_map/all_gather | solution.py:345
  37.2 0.0 collective-permute-done.once
  37.2 0.0 collective-permute-done.1.twice
  37.2 4.6 %shard_map.61 = (f32[1536,128]{1,0:T(8,128)}, f32[4,8,24]{2,1,0:T(8,128)}) custom-call(f32[2,576,128]{2,1,0:T(8,128)S(1)} %bitcast.25, f32[1536,128]{1,0:T(8,128)S(1)} %bitcast.24, f32[4,6,8,256]{3,2,1,0:T(8,128)S(1)} %collective-permute-done.once, f32[4,6,8,256]{3,2,1,0:T(8,128)S(1)} %collective-permute-done.1.twice), custom_call_target="tpu_custom_call" | custom-call | tf_op jit(solution)/shard_map/pallas_call | solution.py:358
Async XLA Ops:
  0.6 25.7 %copy-start = (f32[8,4,24,256]{3,2,1,0:T(8,128)S(1)}, f32[8,4,24,256]{3,2,1,0:T(8,128)}, u32[]{:S(2)}) copy-start(f32[8,4,24,256]{3,2,1,0:T(8,128)} %param.4) | copy-start | bytes 2359300
  10.8 24.2 %all-to-all-start = ((f32[32,1,2304]{2,1,0:T(1,128)}), f32[32,1,2304]{2,1,0:T(1,128)S(1)}, u32[]{:S(2)}, u32[]{:S(2)}) async-start(f32[32,1,2304]{2,1,0:T(1,128)} %bitcast.7), calls=%async_computation | async-start | bytes 589824 | tf_op jit(solution)/shard_map/all_to_all | solution.py:338
  26.6 10.7 %collective-permute-start = (f32[4,6,8,256]{3,2,1,0:T(8,128)S(1)}, f32[4,6,8,256]{3,2,1,0:T(8,128)S(1)}, u32[]{:S(2)}, u32[]{:S(2)}) collective-permute-start(f32[4,6,8,256]{3,2,1,0:T(8,128)S(1)} %get-tuple-element.6), channel_id=1, source_target_pairs={{0,1},{2,3},{4,5},{6,7},{8,9},{10,11},{12,13},{14,15},{1,0},{3,2},... | collective-permute-start | bytes 589832 | tf_op jit(solution)/shard_map/ppermute | solution.py:313
  28.5 8.7 %collective-permute-start.1 = (f32[4,6,8,256]{3,2,1,0:T(8,128)S(1)}, f32[4,6,8,256]{3,2,1,0:T(8,128)S(1)}, u32[]{:S(2)}, u32[]{:S(2)}) collective-permute-start(f32[4,6,8,256]{3,2,1,0:T(8,128)S(1)} %get-tuple-element.7), channel_id=1, source_target_pairs={{1,2},{3,4},{5,6},{7,8},{9,10},{11,12},{13,14},{2,1},{4,3},{6,5},{... | collective-permute-start | bytes 589832 | tf_op jit(solution)/shard_map/ppermute | solution.py:313

commit v8 on v7

--- a/solution.py
+++ b/solution.py
@@ -121,7 +121,7 @@
 
 
 def sweeps(
-    gathered, tracers, once, twice, out, thick_out, fields, mid, weights, ends, turned
+    gathered, tracers, twice, once, out, thick_out, fields, mid, weights, ends, turned
 ):
     space = lax.axis_index("space")
     tracer = lax.axis_index("tracer")
@@ -368,7 +368,7 @@
             pltpu.VMEM((COLS, LEV * SPAN), jnp.float32),
         ],
         compiler_params=PARAMS,
-    )(gathered, flat, once, twice)
+    )(gathered, flat, twice, once)
     return from_tile_rows(values), turn(thick)
 
 

time: 42.2 us -> 42.2 us (level)
  no operation moved by 1% of the time
where the time goes in v8:
time: 42.2 us; the launch traced here: 41.9 us
  starting transfers between devices  18.1 us (43%)
  blocking collectives  10.6 us (25%)
  waiting for transfers between devices  5.84 us (14%)
  Pallas kernels  5.82 us (14%)
  other arithmetic  0.83 us (2%)
  between operations  0.68 us (2%)
    all_to_all x1, starting transfers between devices, per_device(): lax.all_to_all(copies.reshape(count, 1, SHARE * 128), ('tracer', 'space')...  15.5 us
    all_gather x1, blocking collectives, per_device(): pair = lax.all_gather(fields, 'tracer', axis_index_groups=same_chip)  8.39 us
    all_to_all x1, waiting for transfers between devices, per_device(): lax.all_to_all(copies.reshape(count, 1, SHARE * 128), ('tracer', 'space')...  5.83 us
    pallas_call x1, Pallas kernels, per_device(): pl.pallas_call(sweeps, out_shape=[shape(TR * LEV * ROWS * 2, 128), shape(...  4.62 us
    ppermute x2, starting transfers between devices, swap(): return lax.ppermute(block, 'space', pairs + [(b, a) for a, b in pairs])  2.59 us
    all_gather x1, blocking collectives, per_device(): gathered = lax.all_gather(gathered, 'tracer', axis_index_groups=same_chip)  2.22 us
    pallas_call x1, Pallas kernels, per_device(): pl.pallas_call(spread, out_shape=shape(count * SHARE, 128), in_specs=[VME...  0.98 us
  transfers between devices with their start and end apart: 3, of which 1 were waited for; matrix products, arithmetic and copies ran while one was open for 0% of the time, Pallas kernels for 1%

profile of v8, /device:TPU:1, one launch (start us, length us, event | category | flops | bytes accessed | tf_op | source)
XLA Modules:
  0.0 41.9 jit_solution(7054630696905296073)
XLA Ops:
  0.6 0.0 copy-start
  0.6 0.8 %pad_maximum_fusion = f32[3,4,8,24]{3,2,1,0:T(8,128)S(1)} fusion(f32[1,4,8,24]{3,2,1,0:T(8,128)} %bitcast.27, f32[1,4,8,24]{3,2,1,0:T(8,128)} %bitcast.28, f32[1,4,8,24]{3,2,1,0:T(8,128)} %bitcast.29), kind=kLoop, calls=%fused_computation | loop fusion | flops 4608 | bytes 18432 | tf_op jit(solution)/shard_map/stack | solution.py:319
  1.5 8.4 %all-gather = f32[6,4,8,24]{3,2,1,0:T(8,128)S(1)} all-gather(f32[3,4,8,24]{3,2,1,0:T(8,128)S(1)} %pad_maximum_fusion), channel_id=2, replica_groups={{0,16},{32,48},{64,80},{96,112},{128,144},{160,176},{192,208},{224,240}..., dimensions={0}, use_global_device_ids=true | all-gather | bytes 27648 | tf_op jit(solution)/shard_map/all_gather | solution.py:321
  9.9 1.0 %shard_map.59 = f32[576,128]{1,0:T(8,128)} custom-call(f32[2,3,4,8,24]{4,3,2,1,0:T(8,128)S(1)} %bitcast.26), custom_call_target="tpu_custom_call" | custom-call | tf_op jit(solution)/shard_map/pallas_call | solution.py:322
  10.8 15.5 %all-to-all-start = ((f32[32,1,2304]{2,1,0:T(1,128)}), f32[32,1,2304]{2,1,0:T(1,128)S(1)}, u32[]{:S(2)}, u32[]{:S(2)}) async-start(f32[32,1,2304]{2,1,0:T(1,128)} %bitcast.7), calls=%async_computation | async-start | bytes 589824 | tf_op jit(solution)/shard_map/all_to_all | solution.py:338
  26.3 0.0 copy-done
  26.4 0.2 shard_map.60
  26.6 0.7 %collective-permute-start = (f32[4,6,8,256]{3,2,1,0:T(8,128)S(1)}, f32[4,6,8,256]{3,2,1,0:T(8,128)S(1)}, u32[]{:S(2)}, u32[]{:S(2)}) collective-permute-start(f32[4,6,8,256]{3,2,1,0:T(8,128)S(1)} %get-tuple-element.6), channel_id=1, source_target_pairs={{1,2},{3,4},{5,6},{7,8},{9,10},{11,12},{13,14},{2,1},{4,3},{6,5},{... | collective-permute-start | bytes 589832 | tf_op jit(solution)/shard_map/ppermute | solution.py:313
  27.3 1.9 %collective-permute-start.1 = (f32[4,6,8,256]{3,2,1,0:T(8,128)S(1)}, f32[4,6,8,256]{3,2,1,0:T(8,128)S(1)}, u32[]{:S(2)}, u32[]{:S(2)}) collective-permute-start(f32[4,6,8,256]{3,2,1,0:T(8,128)S(1)} %get-tuple-element.7), channel_id=1, source_target_pairs={{0,1},{2,3},{4,5},{6,7},{8,9},{10,11},{12,13},{14,15},{1,0},{3,2},... | collective-permute-start | bytes 589832 | tf_op jit(solution)/shard_map/ppermute | solution.py:313
  29.2 5.8 %all-to-all-done = f32[32,1,2304]{2,1,0:T(1,128)S(1)} async-done(((f32[32,1,2304]{2,1,0:T(1,128)}), f32[32,1,2304]{2,1,0:T(1,128)S(1)}, u32[]{:S(2)}, u32[]{:S(2)}) %all-to-all-start) | async-done | bytes 294944 | tf_op jit(solution)/shard_map/all_to_all | solution.py:338
  35.0 2.2 %all-gather.1 = f32[64,1,2304]{2,1,0:T(1,128)S(1)} all-gather(f32[32,1,2304]{2,1,0:T(1,128)S(1)} %all-to-all-done), channel_id=3, replica_groups={{0,16},{32,48},{64,80},{96,112},{128,144},{160,176},{192,208},{224,240}..., dimensions={0}, use_global_device_ids=true | all-gather | bytes 884736 | tf_op jit(solution)/shard_map/all_gather | solution.py:345
  37.2 0.0 collective-permute-done.twice
  37.2 0.0 collective-permute-done.1.once
  37.2 4.6 %shard_map.61 = (f32[1536,128]{1,0:T(8,128)}, f32[4,8,24]{2,1,0:T(8,128)}) custom-call(f32[2,576,128]{2,1,0:T(8,128)S(1)} %bitcast.25, f32[1536,128]{1,0:T(8,128)S(1)} %bitcast.24, f32[4,6,8,256]{3,2,1,0:T(8,128)S(1)} %collective-permute-done.twice, f32[4,6,8,256]{3,2,1,0:T(8,128)S(1)} %collective-permute-done.1.once), custom_call_target="tpu_custom_call" | custom-call | tf_op jit(solution)/shard_map/pallas_call | solution.py:358
Async XLA Ops:
  0.6 25.7 %copy-start = (f32[8,4,24,256]{3,2,1,0:T(8,128)S(1)}, f32[8,4,24,256]{3,2,1,0:T(8,128)}, u32[]{:S(2)}) copy-start(f32[8,4,24,256]{3,2,1,0:T(8,128)} %param.4) | copy-start | bytes 2359300
  10.8 24.2 %all-to-all-start = ((f32[32,1,2304]{2,1,0:T(1,128)}), f32[32,1,2304]{2,1,0:T(1,128)S(1)}, u32[]{:S(2)}, u32[]{:S(2)}) async-start(f32[32,1,2304]{2,1,0:T(1,128)} %bitcast.7), calls=%async_computation | async-start | bytes 589824 | tf_op jit(solution)/shard_map/all_to_all | solution.py:338
  26.6 10.7 %collective-permute-start = (f32[4,6,8,256]{3,2,1,0:T(8,128)S(1)}, f32[4,6,8,256]{3,2,1,0:T(8,128)S(1)}, u32[]{:S(2)}, u32[]{:S(2)}) collective-permute-start(f32[4,6,8,256]{3,2,1,0:T(8,128)S(1)} %get-tuple-element.6), channel_id=1, source_target_pairs={{1,2},{3,4},{5,6},{7,8},{9,10},{11,12},{13,14},{2,1},{4,3},{6,5},{... | collective-permute-start | bytes 589832 | tf_op jit(solution)/shard_map/ppermute | solution.py:313
  27.3 10.0 %collective-permute-start.1 = (f32[4,6,8,256]{3,2,1,0:T(8,128)S(1)}, f32[4,6,8,256]{3,2,1,0:T(8,128)S(1)}, u32[]{:S(2)}, u32[]{:S(2)}) collective-permute-start(f32[4,6,8,256]{3,2,1,0:T(8,128)S(1)} %get-tuple-element.7), channel_id=1, source_target_pairs={{0,1},{2,3},{4,5},{6,7},{8,9},{10,11},{12,13},{14,15},{1,0},{3,2},... | collective-permute-start | bytes 589832 | tf_op jit(solution)/shard_map/ppermute | solution.py:313

commit v9 on v7

--- a/solution.py
+++ b/solution.py
@@ -342,8 +342,8 @@
         0,
         axis_index_groups=members,
     )
+    gathered = gathered.reshape(count * SHARE, 128)
     gathered = lax.all_gather(gathered, "tracer", axis_index_groups=same_chip)
-    gathered = gathered.reshape(2, count * SHARE, 128)
 
     flat = tile_rows(tracers)
     once, twice = pl.pallas_call(

time: 42.2 us -> 42.2 us (level)
  no operation moved by 1% of the time
where the time goes in v9:
time: 42.2 us; the launch traced here: 41.9 us
  starting transfers between devices  18.1 us (43%)
  blocking collectives  10.6 us (25%)
  waiting for transfers between devices  5.84 us (14%)
  Pallas kernels  5.82 us (14%)
  other arithmetic  0.83 us (2%)
  between operations  0.68 us (2%)
    all_to_all x1, starting transfers between devices, per_device(): lax.all_to_all(copies.reshape(count, 1, SHARE * 128), ('tracer', 'space')...  15.5 us
    all_gather x1, blocking collectives, per_device(): pair = lax.all_gather(fields, 'tracer', axis_index_groups=same_chip)  8.39 us
    all_to_all x1, waiting for transfers between devices, per_device(): lax.all_to_all(copies.reshape(count, 1, SHARE * 128), ('tracer', 'space')...  5.83 us
    pallas_call x1, Pallas kernels, per_device(): pl.pallas_call(sweeps, out_shape=[shape(TR * LEV * ROWS * 2, 128), shape(...  4.62 us
    ppermute x2, starting transfers between devices, swap(): return lax.ppermute(block, 'space', pairs + [(b, a) for a, b in pairs])  2.59 us
    all_gather x1, blocking collectives, per_device(): gathered = lax.all_gather(gathered, 'tracer', axis_index_groups=same_chip)  2.22 us
    pallas_call x1, Pallas kernels, per_device(): pl.pallas_call(spread, out_shape=shape(count * SHARE, 128), in_specs=[VME...  0.98 us
  transfers between devices with their start and end apart: 3, of which 1 were waited for; matrix products, arithmetic and copies ran while one was open for 0% of the time, Pallas kernels for 1%

profile of v9, /device:TPU:1, one launch (start us, length us, event | category | flops | bytes accessed | tf_op | source)
XLA Modules:
  0.0 41.9 jit_solution(10349958721830608413)
XLA Ops:
  0.6 0.0 copy-start
  0.6 0.8 %pad_maximum_fusion = f32[3,4,8,24]{3,2,1,0:T(8,128)S(1)} fusion(f32[1,4,8,24]{3,2,1,0:T(8,128)} %bitcast.27, f32[1,4,8,24]{3,2,1,0:T(8,128)} %bitcast.28, f32[1,4,8,24]{3,2,1,0:T(8,128)} %bitcast.29), kind=kLoop, calls=%fused_computation | loop fusion | flops 4608 | bytes 18432 | tf_op jit(solution)/shard_map/stack | solution.py:319
  1.5 8.4 %all-gather = f32[6,4,8,24]{3,2,1,0:T(8,128)S(1)} all-gather(f32[3,4,8,24]{3,2,1,0:T(8,128)S(1)} %pad_maximum_fusion), channel_id=2, replica_groups={{0,16},{32,48},{64,80},{96,112},{128,144},{160,176},{192,208},{224,240}..., dimensions={0}, use_global_device_ids=true | all-gather | bytes 27648 | tf_op jit(solution)/shard_map/all_gather | solution.py:321
  9.9 1.0 %shard_map.59 = f32[576,128]{1,0:T(8,128)} custom-call(f32[2,3,4,8,24]{4,3,2,1,0:T(8,128)S(1)} %bitcast.25), custom_call_target="tpu_custom_call" | custom-call | tf_op jit(solution)/shard_map/pallas_call | solution.py:322
  10.8 15.5 %all-to-all-start = ((f32[32,1,2304]{2,1,0:T(1,128)}), f32[32,1,2304]{2,1,0:T(1,128)S(1)}, u32[]{:S(2)}, u32[]{:S(2)}) async-start(f32[32,1,2304]{2,1,0:T(1,128)} %bitcast.7), calls=%async_computation | async-start | bytes 589824 | tf_op jit(solution)/shard_map/all_to_all | solution.py:338
  26.3 0.0 copy-done
  26.4 0.2 shard_map.60
  26.6 1.9 %collective-permute-start = (f32[4,6,8,256]{3,2,1,0:T(8,128)S(1)}, f32[4,6,8,256]{3,2,1,0:T(8,128)S(1)}, u32[]{:S(2)}, u32[]{:S(2)}) collective-permute-start(f32[4,6,8,256]{3,2,1,0:T(8,128)S(1)} %get-tuple-element.6), channel_id=1, source_target_pairs={{0,1},{2,3},{4,5},{6,7},{8,9},{10,11},{12,13},{14,15},{1,0},{3,2},... | collective-permute-start | bytes 589832 | tf_op jit(solution)/shard_map/ppermute | solution.py:313
  28.5 0.7 %collective-permute-start.1 = (f32[4,6,8,256]{3,2,1,0:T(8,128)S(1)}, f32[4,6,8,256]{3,2,1,0:T(8,128)S(1)}, u32[]{:S(2)}, u32[]{:S(2)}) collective-permute-start(f32[4,6,8,256]{3,2,1,0:T(8,128)S(1)} %get-tuple-element.7), channel_id=1, source_target_pairs={{1,2},{3,4},{5,6},{7,8},{9,10},{11,12},{13,14},{2,1},{4,3},{6,5},{... | collective-permute-start | bytes 589832 | tf_op jit(solution)/shard_map/ppermute | solution.py:313
  29.2 5.8 %all-to-all-done = f32[32,1,2304]{2,1,0:T(1,128)S(1)} async-done(((f32[32,1,2304]{2,1,0:T(1,128)}), f32[32,1,2304]{2,1,0:T(1,128)S(1)}, u32[]{:S(2)}, u32[]{:S(2)}) %all-to-all-start) | async-done | bytes 294944 | tf_op jit(solution)/shard_map/all_to_all | solution.py:338
  35.0 2.2 %all_gather.11.gathered = f32[2,576,128]{2,1,0:T(8,128)S(1)} all-gather(f32[1,576,128]{2,1,0:T(8,128)S(1)} %bitcast.26), channel_id=1, replica_groups={{0,16},{32,48},{64,80},{96,112},{128,144},{160,176},{192,208},{224,240}..., dimensions={0}, use_global_device_ids=true | all-gather | bytes 884736 | tf_op jit(solution)/shard_map/all_gather | solution.py:346
  37.2 0.0 collective-permute-done.once
  37.2 0.0 collective-permute-done.1.twice
  37.2 4.6 %shard_map.61 = (f32[1536,128]{1,0:T(8,128)}, f32[4,8,24]{2,1,0:T(8,128)}) custom-call(f32[2,576,128]{2,1,0:T(8,128)S(1)} %all_gather.11.gathered, f32[1536,128]{1,0:T(8,128)S(1)} %bitcast.24, f32[4,6,8,256]{3,2,1,0:T(8,128)S(1)} %collective-permute-done.once, f32[4,6,8,256]{3,2,1,0:T(8,128)S(1)} %collective-permute-done.1.twice), custom_call_target="tpu_custom_call" | custom-call | tf_op jit(solution)/shard_map/pallas_call | solution.py:358
Async XLA Ops:
  0.6 25.7 %copy-start = (f32[8,4,24,256]{3,2,1,0:T(8,128)S(1)}, f32[8,4,24,256]{3,2,1,0:T(8,128)}, u32[]{:S(2)}) copy-start(f32[8,4,24,256]{3,2,1,0:T(8,128)} %param.4) | copy-start | bytes 2359300
  10.8 24.2 %all-to-all-start = ((f32[32,1,2304]{2,1,0:T(1,128)}), f32[32,1,2304]{2,1,0:T(1,128)S(1)}, u32[]{:S(2)}, u32[]{:S(2)}) async-start(f32[32,1,2304]{2,1,0:T(1,128)} %bitcast.7), calls=%async_computation | async-start | bytes 589824 | tf_op jit(solution)/shard_map/all_to_all | solution.py:338
  26.6 10.7 %collective-permute-start = (f32[4,6,8,256]{3,2,1,0:T(8,128)S(1)}, f32[4,6,8,256]{3,2,1,0:T(8,128)S(1)}, u32[]{:S(2)}, u32[]{:S(2)}) collective-permute-start(f32[4,6,8,256]{3,2,1,0:T(8,128)S(1)} %get-tuple-element.6), channel_id=1, source_target_pairs={{0,1},{2,3},{4,5},{6,7},{8,9},{10,11},{12,13},{14,15},{1,0},{3,2},... | collective-permute-start | bytes 589832 | tf_op jit(solution)/shard_map/ppermute | solution.py:313
  28.5 8.7 %collective-permute-start.1 = (f32[4,6,8,256]{3,2,1,0:T(8,128)S(1)}, f32[4,6,8,256]{3,2,1,0:T(8,128)S(1)}, u32[]{:S(2)}, u32[]{:S(2)}) collective-permute-start(f32[4,6,8,256]{3,2,1,0:T(8,128)S(1)} %get-tuple-element.7), channel_id=1, source_target_pairs={{1,2},{3,4},{5,6},{7,8},{9,10},{11,12},{13,14},{2,1},{4,3},{6,5},{... | collective-permute-start | bytes 589832 | tf_op jit(solution)/shard_map/ppermute | solution.py:313
